TPU v7x, 128 devices: a whole 4x4x4 slice. The times are simulated.
128 devices in a mesh: row: 16 (over z, x_hi, core), col: 8 (over y, x_lo).
Axes of the slice: x: 4 (x_hi: 2, x_lo: 2; x = x_hi * 2 + x_lo), y: 4, z: 4, core: 2. Of those that a mesh axis runs over, the one named last changes fastest.
Arguments:
- pair_state: float32 [768, 768, 128], P('row', 'col'), may hold values from -120 to 120
- pair_mask: int32 [768, 768], P('row', 'col'), may hold values 0 or 1
- chain_ids: int32 [768], replicated, may hold values from 0 to 5, never falling along the last dimension, each value on 1 to 256 neighbouring positions
- ln_gain: float32 [2, 128], replicated, may hold values from 0.25 to 1.75
- w_proj: float32 [2, 128, 512], replicated, may hold values from -0.5 to 0.5
- w_bias: float32 [2, 128, 4], replicated, may hold values from -35.35534 to 35.35534
- w_out: float32 [2, 128, 128], replicated, may hold values from -1.8 to 1.8
- chain_gain: float32 [2, 4], replicated, may hold values from -4 to 4
Outputs:
- pair_out: float32 [768, 768, 128], P('row', 'col')
All inputs are finite; a program needn't handle non-finite values. No bound on the sum of `pair_mask` on one device may be relied on, other than what follows from the above.
Results may differ from a plain program's by a relative error of at most 0.0003.
Values sent between devices are 32-bit elements; how exact they have to be, the bound alone decides.
No kernel may reach another device: no remote copies, remote signals or barrier semaphores. Data moves between devices by JAX's collectives and lax.ppermute only.
A program may use at most 128 MiB of HBM per device.

v0:
```python
import jax
import jax.numpy as jnp
from jax import lax
from jax.sharding import PartitionSpec as P


def layer_norm(values, scales):
    average = jnp.mean(values, axis=-1, keepdims=True)
    centred = values - average
    variance = jnp.mean(centred * centred, axis=-1, keepdims=True)
    return centred * lax.rsqrt(variance + 1e-05) * scales


def attend(normed_line, mask_line, bias_plane, w_proj, w_out, keys_first):
    width = normed_line.shape[1]
    head_count = bias_plane.shape[0]
    head_size = width // head_count
    projected = jnp.dot(normed_line, w_proj, precision=lax.Precision.HIGHEST)
    query_proj = projected[:, :width].reshape(-1, head_count, head_size) * head_size ** (-0.5)
    key_proj = projected[:, width : 2 * width].reshape(-1, head_count, head_size)
    value_proj = projected[:, 2 * width : 3 * width].reshape(-1, head_count, head_size)
    gate_proj = projected[:, 3 * width :]
    mask_add = (mask_line - 1.0) * 1000000000.0
    if keys_first:
        scores = jnp.einsum("khd,ahd->hka", key_proj, query_proj, precision=lax.Precision.HIGHEST)
        scores = scores + bias_plane + mask_add[None, :, None]
        attention = jax.nn.softmax(scores, axis=1)
        mixed_out = jnp.einsum(
            "hka,khd->ahd", attention, value_proj, precision=lax.Precision.HIGHEST
        )
    else:
        scores = jnp.einsum("jhd,khd->hjk", query_proj, key_proj, precision=lax.Precision.HIGHEST)
        scores = scores + bias_plane + mask_add[None, None, :]
        attention = jax.nn.softmax(scores, axis=-1)
        mixed_out = jnp.einsum(
            "hjk,khd->jhd", attention, value_proj, precision=lax.Precision.HIGHEST
        )
    mixed_out = mixed_out.reshape(-1, width)
    return jnp.dot(jax.nn.sigmoid(gate_proj) * mixed_out, w_out, precision=lax.Precision.HIGHEST)


def local_bias(normed, w_bias):
    return jnp.einsum("jkc,ch->hjk", normed, w_bias, precision=lax.Precision.HIGHEST)


def end_columns(column_normed, column_mask, bias_plane, w_proj, w_out):
    lines = jnp.moveaxis(column_normed, 1, 0)
    masks = jnp.transpose(column_mask)
    update = lax.map(
        lambda inputs: attend(inputs[0], inputs[1], bias_plane, w_proj, w_out, True), (lines, masks)
    )
    return jnp.moveaxis(update, 0, 1)


def local(pair_state, pair_mask, chain_ids, ln_gain, w_proj, w_bias, w_out, chain_gain):
    mask_float = pair_mask.astype(jnp.float32)
    same_chain = (chain_ids[:, None] == chain_ids[None, :]).astype(jnp.float32)
    rows_pair, rows_mask = (
        lax.all_to_all(pair_state, "col", split_axis=0, concat_axis=1, tiled=True),
        lax.all_to_all(mask_float, "col", split_axis=0, concat_axis=1, tiled=True),
    )
    normed = layer_norm(rows_pair, ln_gain[0])
    start_plane = lax.all_gather(local_bias(normed, w_bias[0]), ("row", "col"), axis=1, tiled=True)
    start_plane = start_plane + chain_gain[0][:, None, None] * same_chain[None]
    update = lax.map(
        lambda inputs: attend(inputs[0], inputs[1], start_plane, w_proj[0], w_out[0], False),
        (normed, rows_mask),
    )
    first_pair = rows_pair + update
    end_normed = layer_norm(first_pair, ln_gain[1])
    end_plane = lax.all_gather(
        local_bias(end_normed, w_bias[1]), ("row", "col"), axis=1, tiled=True
    )
    end_plane = end_plane + chain_gain[1][:, None, None] * same_chain[None]
    tile_pair = lax.all_to_all(first_pair, "col", split_axis=1, concat_axis=0, tiled=True)
    tile_normed = layer_norm(tile_pair, ln_gain[1])
    column_normed, column_mask = (
        lax.all_to_all(tile_normed, "row", split_axis=1, concat_axis=0, tiled=True),
        lax.all_to_all(mask_float, "row", split_axis=1, concat_axis=0, tiled=True),
    )
    end_update = end_columns(column_normed, column_mask, end_plane, w_proj[1], w_out[1])
    returned = lax.all_to_all(end_update, "row", split_axis=0, concat_axis=1, tiled=True)
    return tile_pair + returned


def solution(mesh):
    return jax.shard_map(
        local,
        mesh=mesh,
        in_specs=(P("row", "col", None), P("row", "col"), P(), P(), P(), P(), P(), P()),
        out_specs=P("row", "col", None),
        check_vma=False,
    )
```

profile of v0, /device:TPU:1, one launch (start us, length us, event | category | flops | bytes accessed | tf_op | source)
XLA Modules:
  0.0 1259.8 jit_solution(13603162179226990778)
XLA Ops:
  12.7 28.8 %all-to-all-done = f32[48,96,128]{2,1,0:T(8,128)S(1)} async-done(((f32[48,96,128]{2,1,0:T(8,128)}), f32[48,96,128]{2,1,0:T(8,128)S(1)}, u32[]{:S(2)}, u32[]{:S(2)}) %all-to-all-start) | async-done | bytes 2359328 | tf_op jit(solution)/shard_map/all_to_all | solution.py:59
  68.4 302.7 %all-gather.3.cloned.1.call-done = f32[4,768,768]{2,0,1:T(4,128)} async-done(((f32[4,6,768]{2,0,1:T(4,128)}), f32[4,768,768]{2,0,1:T(4,128)}) %all-gather.3.cloned.1.call-update) | async-done | bytes 9437200 | tf_op jit(solution)/shard_map/all_gather | solution.py:63
  371.1 11.2 multiply_add_fusion.1
  382.3 11.9 copy.57
  396.1 230.9 %while.24 = (s32[]{:T(128)}, f32[6,768,128]{2,0,1:T(8,128)}, f32[6,768,128]{2,0,1:T(8,128)}, f32[2,128,512]{2,1,0:T(8,128)}, f32[4,768,768]{1,2,0:T(8,128)}, /*i...) while((s32[]{:T(128)}, f32[6,768,128]{2,0,1:T(8,128)}, f32[6,768,128]{2,0,1:T(8,128)}, ...), condition=%wide.region_5.6_spmd, body=%wide.region_2.5_spmd.sunk | while | flops 2583916032 | bytes 48108676 | solution.py:65
  402.0 11.2 fusion.95
  422.0 11.4 dynamic_update_slice.15
  439.0 11.2 fusion.95
  458.9 11.4 dynamic_update_slice.15
  475.9 11.2 fusion.95
  495.8 11.4 dynamic_update_slice.15
  512.8 11.2 fusion.95
  532.8 11.4 dynamic_update_slice.15
  549.7 11.2 fusion.95
  569.7 11.4 dynamic_update_slice.15
  586.6 11.2 fusion.95
  606.6 11.4 dynamic_update_slice.15
  647.4 41.5 %all-to-all-done.2 = f32[6,768,128]{2,0,1:T(8,128)S(1)} async-done(((f32[6,768,128]{2,0,1:T(8,128)}), f32[6,768,128]{2,0,1:T(8,128)S(1)}, u32[]{:S(2)}, u32[]{:S(2)}) %all-to-all-start.2) | async-done | bytes 2359328 | tf_op jit(solution)/shard_map/all_to_all | solution.py:75
  719.3 30.1 %all-to-all-done.3 = f32[48,96,128]{2,0,1:T(8,128)} async-done(((f32[48,96,128]{2,0,1:T(8,128)}), f32[48,96,128]{2,0,1:T(8,128)}, u32[]{:S(2)}, u32[]{:S(2)}) %all-to-all-start.3) | async-done | bytes 2359328 | tf_op jit(solution)/shard_map/all_to_all | solution.py:78
  752.9 245.7 %all-gather.5.cloned.1.call-done = f32[4,768,768]{2,0,1:T(4,128)} async-done(((f32[4,6,768]{2,0,1:T(4,128)}), f32[4,768,768]{2,0,1:T(4,128)}) %all-gather.5.cloned.1.call-update) | async-done | bytes 9437200 | tf_op jit(solution)/shard_map/all_gather | solution.py:71
  1011.4 190.7 %while.25 = (s32[]{:T(128)}, f32[6,768,128]{2,0,1:T(8,128)S(1)}, f32[6,768,128]{2,1,0:T(8,128)}, f32[128,512]{1,0:T(8,128)}, f32[4,768,768]{2,1,0:T(8,128)}, /*i...) while((s32[]{:T(128)}, f32[6,768,128]{2,0,1:T(8,128)S(1)}, f32[6,768,128]{2,1,0:T(8,128)}, ...), condition=%wide.region_13.14_spmd, body=%wide.region_10.13_spmd.sunk | while | flops 2583916032 | bytes 47060608 | solution.py:49
  1015.0 11.2 fusion.109
  1034.9 8.4 dynamic_update_slice.16
  1046.7 11.2 fusion.109
  1066.7 8.4 dynamic_update_slice.16
  1078.5 11.2 fusion.109
  1110.2 11.2 fusion.109
  1130.2 8.4 dynamic_update_slice.16
  1142.0 11.2 fusion.109
  1173.7 11.2 fusion.109
  1193.7 8.4 dynamic_update_slice.16
  1202.1 46.7 %all_to_all.110 = f32[768,6,128]{2,1,0:T(8,128)S(1)} all-to-all(f32[768,6,128]{2,1,0:T(8,128)S(1)} %bitcast.180), channel_id=1, replica_groups=mesh['row'=16,'col'=8] {'row'}, dimensions={0} | all-to-all | bytes 4718592 | tf_op jit(solution)/shard_map/all_to_all | solution.py:82
  (209 shorter events, 279.9 us)
Async XLA Ops:
  6.5 6.1 copy-start.15
  6.5 35.0 %all-to-all-start = ((f32[48,96,128]{2,1,0:T(8,128)}), f32[48,96,128]{2,1,0:T(8,128)S(1)}, u32[]{:S(2)}, u32[]{:S(2)}) async-start(f32[48,96,128]{2,1,0:T(8,128)} %param.12), calls=%async_computation | async-start | bytes 4718592 | tf_op jit(solution)/shard_map/all_to_all | solution.py:59
  12.6 358.5 %all-gather.3.cloned.1.call-start = ((), (), s32[]{:S(2)}) async-start(), calls=%async_computation.6 | async-start | bytes 9510912 | tf_op jit(solution)/shard_map/all_gather | solution.py:63
  48.3 3.4 copy-start.12
  48.4 7.9 copy-start.13
  48.8 9.1 copy-start.16
  51.8 11.6 copy-start.10
  52.4 8.9 all-to-all-start.1
  56.2 942.3 %all-gather.5.cloned.1.call-start = ((), (), s32[]{:S(2)}) async-start(), calls=%async_computation.7 | async-start | bytes 9510912 | tf_op jit(solution)/shard_map/all_gather | solution.py:71
  63.4 1.7 copy-start
  65.0 306.1 %copy-start.2 = (f32[768,768]{1,0:T(8,128)S(1)}, f32[768,768]{1,0:T(8,128)}, u32[]{:S(2)}) copy-start(f32[768,768]{1,0:T(8,128)} %compare_convert_fusion) | copy-start | bytes 7077892
  396.1 231.0 %copy-start.1 = (f32[8,6,96,128]{3,1,2,0:T(8,128)S(1)}, f32[8,6,96,128]{3,1,2,0:T(8,128)}, u32[]{:S(2)}) copy-start(f32[8,6,96,128]{3,1,2,0:T(8,128)} %copy-done) | copy-start | bytes 7077892
  414.5 6.7 copy-start.8
  451.4 6.7 copy-start.8
  488.4 6.7 copy-start.8
  525.3 6.7 copy-start.8
  562.2 6.7 copy-start.8
  599.1 6.7 copy-start.8
  642.9 3.7 copy-start.11
  642.9 46.0 %all-to-all-start.2 = ((f32[6,768,128]{2,0,1:T(8,128)}), f32[6,768,128]{2,0,1:T(8,128)S(1)}, u32[]{:S(2)}, u32[]{:S(2)}) async-start(f32[6,768,128]{2,0,1:T(8,128)} %get-tuple-element.284), calls=%async_computation.2 | async-start | bytes 6291456 | tf_op jit(solution)/shard_map/all_to_all | solution.py:75
  688.8 19.6 %all-to-all-start.4 = ((f32[16,1,288]{2,1,0:T(1,128)}), f32[16,1,288]{2,1,0:T(1,128)S(1)}, u32[]{:S(2)}, u32[]{:S(2)}) async-start(f32[16,1,288]{2,1,0:T(1,128)} %reshape.195), calls=%async_computation.4 | async-start | bytes 49152 | tf_op jit(solution)/shard_map/all_to_all | solution.py:79
  708.5 7.4 copy-start.9
  708.5 8.0 copy-start.6
  708.5 41.0 %all-to-all-start.3 = ((f32[48,96,128]{2,0,1:T(8,128)}), f32[48,96,128]{2,0,1:T(8,128)}, u32[]{:S(2)}, u32[]{:S(2)}) async-start(f32[48,96,128]{2,0,1:T(8,128)} %copy.63), calls=%async_computation.3 | async-start | bytes 4718592 | tf_op jit(solution)/shard_map/all_to_all | solution.py:78
  715.8 282.7 %copy-start.3 = (f32[768,768]{1,0:T(8,128)S(1)}, f32[768,768]{1,0:T(8,128)}, u32[]{:S(2)}) copy-start(f32[768,768]{1,0:T(8,128)} %compare_convert_fusion) | copy-start | bytes 7077892
  1027.4 6.7 copy-start.7
  1059.2 6.7 copy-start.7
  1090.9 6.7 copy-start.7
  1122.7 6.7 copy-start.7
  1154.4 6.7 copy-start.7
  1186.2 6.7 copy-start.7
  1248.8 1.7 copy-start.5
  (2 other events, 2.1 us)
Sparse Core Ops, SparseCore 0:
  51.9 319.1 all-gather.2
  643.0 355.5 all-gather.4
where the time goes:
time: 1270 us; the launch traced here: 1260 us
  waiting for transfers between devices  652 us (51%)
  matrix products  258 us (20%)
  local copies, waits for them, and re-layouts  172 us (14%)
  other arithmetic  79.7 us (6%)
  blocking collectives  46.7 us (4%)
  starting transfers between devices  26.9 us (2%)
  between operations  14.2 us (1%)
    all_gather x1, waiting for transfers between devices, local(): lax.all_gather(local_bias(normed, w_bias[0]), ('row', 'col'), axis=1, til...  303 us
    all_gather x1, waiting for transfers between devices, local(): lax.all_gather(local_bias(end_normed, w_bias[1]), ('row', 'col'), axis=1,...  246 us
    dynamic_update_slice x12, local copies, waits for them, and re-layouts, local(): lax.map(lambda inputs: attend(inputs[0], inputs[1], start_plane, w_proj[0...  119 us
    dot_general x6, matrix products, attend(): jnp.einsum('jhd,khd->hjk', query_proj, key_proj, precision=lax.Precision....  67.3 us
    dot_general x6, matrix products, attend(): jnp.einsum('khd,ahd->hka', key_proj, query_proj, precision=lax.Precision....  67.1 us
    all_to_all x1, blocking collectives, local(): lax.all_to_all(end_update, 'row', split_axis=0, concat_axis=1, tiled=True)  46.7 us
    all_to_all x1, waiting for transfers between devices, local(): lax.all_to_all(first_pair, 'col', split_axis=1, concat_axis=0, tiled=True)  41.5 us
    dot_general x6, matrix products, attend(): jnp.einsum('hjk,khd->jhd', attention, value_proj, precision=lax.Precision...  39.2 us
  transfers between devices with their start and end apart: 7, of which 6 were waited for; matrix products, arithmetic and copies ran while one was open for 2% of the time, Pallas kernels for 0%

commit v1 on v0

v1 whole, which is shorter than its diff:
```python
import functools
import jax
import jax.numpy as jnp
from jax import lax
from jax.experimental import pallas as pl
from jax.experimental.pallas import tpu as pltpu
from jax.sharding import Mesh, PartitionSpec as P

N = 768
HEADS = 4
LINES = 6
SLOT = 40
LOG2E = 1.4426950408889634
F32 = jnp.float32
BF16 = jnp.bfloat16
ROW = ("z", "x_hi", "core")
COL = ("y", "x_lo")
EVERY = ROW + COL
GATHER = ("z", "x_hi", "x_lo", "y", "core")
NT = (((1,), (1,)), ((), ()))
TN = (((0,), (0,)), ((), ()))


def split(values):
    high = values.astype(BF16)
    return high, (values - high.astype(F32)).astype(BF16)


def layer_norm(values, scales):
    average = jnp.mean(values, axis=-1, keepdims=True)
    centred = values - average
    variance = jnp.mean(centred * centred, axis=-1, keepdims=True)
    return centred * lax.rsqrt(variance + 1e-05) * scales


def halves(values):
    return values[:, :128] + values[:, 128:]


def gathered_place(row, col):
    return (row // 2) * 16 + (col % 2) * 8 + (col // 2) * 2 + row % 2


def order_bias(gathered, bias, keys_by_col):
    def step(outer, _):
        for part in range(4):
            if keys_by_col:
                owners = [gathered_place(part * 4 + t, outer) for t in range(4)]
            else:
                owners = [gathered_place(outer * 2 + part // 2, (part % 2) * 4 + t) for t in range(4)]
            blocks = [
                gathered[pl.ds(pl.multiple_of(owner * 24, 8), 24), :] for owner in owners
            ]
            start = pl.multiple_of(outer * 96 + part * 24, 8)
            for head in range(HEADS):
                rows = [block[head * LINES : (head + 1) * LINES] for block in blocks]
                bias[head, pl.ds(start, 24), :] = jnp.concatenate(rows, axis=0)
        return 0

    lax.fori_loop(0, 8, step, 0)


def attend(x, mask, bias, w_query, w_key, w_value, w_gate, w_out, gain, query, key, value, mixed, gate):
    normed_high, normed_low = split(layer_norm(x, gain))
    normed = jnp.concatenate([normed_high, normed_low], axis=1)

    def turned(weights):
        both = lax.dot_general(weights[...], normed, NT, preferred_element_type=F32)
        return both[:128] + both[128:]

    key_proj = halves(jnp.dot(normed, w_key[...], preferred_element_type=F32))
    query_high, query_low = split(turned(w_query))
    value_high, value_low = split(turned(w_value))
    gate[...] = turned(w_gate)
    block = lax.broadcasted_iota(jnp.int32, (1, 128), 1) // 32
    masked = jnp.broadcast_to(mask - 1.0, (N, 128))
    key_high = key_proj.astype(BF16).astype(F32)
    key_low = pltpu.roll(key_proj - key_high, 64, 1)
    key_again = pltpu.roll(key_high, 32, 1)
    place = lax.broadcasted_iota(jnp.int32, (32, N), 0)
    weight = jnp.where(
        place == 0, 1442840576.0, jnp.where(place == 1, -145408.0, jnp.where(place == 2, -128.0, 0.0))
    ).astype(BF16)
    ones = jnp.ones((16, N), BF16)
    for head in range(HEADS):
        at = [(head + t) % 4 for t in range(4)]
        part = slice(head * 32, (head + 1) * 32)
        key[head] = jnp.where(
            block == at[0],
            key_high,
            jnp.where(block == at[1], key_again, jnp.where(block == at[2], key_low, masked)),
        ).astype(BF16)
        rows = [None] * 4
        rows[at[0]] = query_high[part]
        rows[at[1]] = query_low[part]
        rows[at[2]] = query_high[part]
        rows[at[3]] = weight
        query[head] = jnp.concatenate(rows, axis=0)
        value[head] = jnp.concatenate([value_high[part], value_low[part], ones], axis=0)
    width = 256
    for head in range(HEADS):
        for start in range(0, N, width):
            span = slice(start, start + width)
            scores = jnp.dot(key[head], query[head, :, span], preferred_element_type=F32)
            scores = scores + bias[head, :, span]
            weights = jnp.exp2(scores - jnp.max(scores, axis=0, keepdims=True))
            high, low = split(weights)
            total = jnp.dot(value[head], high, preferred_element_type=F32)
            total = total + jnp.dot(value[head], low, preferred_element_type=F32)
            mixed[head * 32 : (head + 1) * 32, span] = (total[:32] + total[32:64]) / total[64:65]
    gated_high, gated_low = split(jax.nn.sigmoid(gate[...]) * mixed[...])
    gated = jnp.concatenate([gated_high, gated_low], axis=0)
    return halves(lax.dot_general(gated, w_out[...], TN, preferred_element_type=F32))


def start_kernel(
    x_ref, mask_ref, gathered, w_query, w_key, w_value, w_gate, w_out, gain, end_gain, w_bias, chain, same,
    pair_ref, bias_ref, bias, query, key, value, mixed, gate, line,
):
    step = pl.program_id(0)

    @pl.when(step == 0)
    def _():
        order_bias(gathered, bias, True)
        pair_ref[...] = jnp.zeros_like(pair_ref)

    x = x_ref[...].reshape(N, 128)
    update = attend(
        x, mask_ref[0], bias, w_query, w_key, w_value, w_gate, w_out, gain[...], query, key, value, mixed, gate
    )
    first = x + update
    line[...] = first
    for row in range(16):
        for t in range(LINES):
            pair_ref[pl.ds(row * 8 * SLOT + step * LINES + t, 8, stride=SLOT), :] = line[
                pl.ds(row * LINES + t, 8, stride=96), :
            ]
    normed = layer_norm(first, end_gain[...])
    plane = lax.dot_general(
        w_bias[...], normed, NT, precision=lax.Precision.HIGHEST, preferred_element_type=F32
    )
    plane = (plane + chain[:, :1] * same[0]) * LOG2E
    for head in range(HEADS):
        bias_ref[pl.ds(head * LINES + step, 1), :] = plane[head : head + 1]


def end_kernel(
    x_ref, mask_ref, gathered, w_query, w_key, w_value, w_gate, w_out, gain,
    out_ref, bias, query, key, value, mixed, gate, line,
):
    step = pl.program_id(0)

    @pl.when(step == 0)
    def _():
        order_bias(gathered, bias, False)

    for t in range(LINES):
        for group in range(16):
            line[pl.ds(group * 8 * LINES + t, 8, stride=LINES), :] = x_ref[
                pl.ds(group * 8 * SLOT + t * LINES + step, 8, stride=SLOT), :
            ]
    x = line[...]
    update = attend(
        x, mask_ref[0], bias, w_query, w_key, w_value, w_gate, w_out, gain[...], query, key, value, mixed, gate
    )
    out_ref[...] = (x + update).reshape(16, 1, 48, 128)


def whole(shape):
    return pl.BlockSpec(shape, lambda i: (0,) * len(shape), pipeline_mode=pl.Buffered(1))


SCRATCH = [
    pltpu.VMEM((HEADS, N, N), F32),
    pltpu.VMEM((HEADS, 128, N), BF16),
    pltpu.VMEM((HEADS, N, 128), BF16),
    pltpu.VMEM((HEADS, 80, N), BF16),
    pltpu.VMEM((128, N), F32),
    pltpu.VMEM((128, N), F32),
    pltpu.VMEM((N, 128), F32),
]
PARAMS = pltpu.CompilerParams(vmem_limit_bytes=56 * 1024 * 1024)


def doubled(weights):
    high = lax.reduce_precision(weights, 8, 7)
    both = jnp.concatenate([high, weights - high], axis=1)
    return jnp.concatenate([both, both], axis=0).astype(BF16)


def prepared(w_proj, w_out):
    w_query = doubled(w_proj[:, :128] * (32 ** -0.5 * LOG2E)).T
    w_key = doubled(w_proj[:, 128:256])
    w_value = doubled(w_proj[:, 256:384]).T
    w_gate = doubled(w_proj[:, 384:]).T
    return w_query, w_key, w_value, w_gate, doubled(w_out)


def local(pair_state, pair_mask, chain_ids, ln_gain, w_proj, w_bias, w_out, chain_gain):
    row, col = lax.axis_index(ROW), lax.axis_index(COL)
    mask_float = pair_mask.astype(F32)
    rows_pair = lax.all_to_all(pair_state, COL, split_axis=0, concat_axis=0, tiled=True)
    rows_pair = rows_pair.reshape(8, LINES, 96, 128)
    rows_mask = lax.all_to_all(mask_float, COL, split_axis=0, concat_axis=0, tiled=True)
    rows_mask = jnp.transpose(rows_mask.reshape(8, LINES, 96), (1, 0, 2)).reshape(LINES, N, 1)

    normed = layer_norm(pair_state, ln_gain[0])
    tile_bias = jnp.einsum("jkc,ch->hjk", normed, w_bias[0], precision=lax.Precision.HIGHEST)
    ids_row = lax.dynamic_slice(chain_ids, (row * 48,), (48,))
    ids_col = lax.dynamic_slice(chain_ids, (col * 96,), (96,))
    same = (ids_row[:, None] == ids_col[None, :]).astype(F32)
    tile_bias = (tile_bias + chain_gain[0][:, None, None] * same[None]) * LOG2E
    planes = jnp.concatenate([tile_bias, mask_float[None]], axis=0)
    planes = jnp.transpose(planes.reshape(5, 48, 16, LINES), (2, 0, 3, 1))
    planes = lax.all_to_all(planes, ROW, split_axis=0, concat_axis=0, tiled=True)
    planes = jnp.transpose(planes, (1, 2, 0, 3)).reshape(5, LINES, N)
    ends_mask = planes[4].reshape(LINES, N, 1)
    start_bias = lax.all_gather(planes[:4].reshape(24, N), GATHER, axis=0, tiled=True)

    ids_line = lax.dynamic_slice(chain_ids, (row * 48 + col * LINES,), (LINES,))
    same_line = (ids_line[:, None] == chain_ids[None, :]).astype(F32).reshape(LINES, 1, N)
    end_w = jnp.concatenate([w_bias[1].T, jnp.zeros((4, 128), F32)], axis=0)
    chain = jnp.broadcast_to(jnp.concatenate([chain_gain[1], jnp.zeros((4,), F32)])[:, None], (8, 128))
    matrix = whole((256, 256))
    first_pair, end_shard = pl.pallas_call(
        start_kernel,
        grid=(LINES,),
        out_shape=(
            jax.ShapeDtypeStruct((128 * SLOT, 128), F32),
            jax.ShapeDtypeStruct((HEADS * LINES, N), F32),
        ),
        in_specs=[
            pl.BlockSpec((8, 1, 96, 128), lambda i: (0, i, 0, 0)),
            pl.BlockSpec((1, N, 1), lambda i: (i, 0, 0)),
            whole((128 * 24, N)),
            matrix, matrix, matrix, matrix, matrix,
            whole((1, 128)), whole((1, 128)), whole((8, 128)), whole((8, 128)),
            pl.BlockSpec((1, 1, N), lambda i: (i, 0, 0)),
        ],
        out_specs=(whole((128 * SLOT, 128)), whole((HEADS * LINES, N))),
        scratch_shapes=SCRATCH,
        compiler_params=PARAMS,
        name="start_attention",
    )(
        rows_pair, rows_mask, start_bias, *prepared(w_proj[0], w_out[0]),
        ln_gain[0:1], ln_gain[1:2], end_w, chain, same_line,
    )
    end_bias = lax.all_gather(end_shard, GATHER, axis=0, tiled=True)
    columns = lax.all_to_all(
        first_pair.reshape(128, SLOT, 128), EVERY, split_axis=0, concat_axis=0, tiled=True
    ).reshape(128 * SLOT, 128)
    second = pl.pallas_call(
        end_kernel,
        grid=(LINES,),
        out_shape=jax.ShapeDtypeStruct((16, LINES, 48, 128), F32),
        in_specs=[
            whole((128 * SLOT, 128)),
            pl.BlockSpec((1, N, 1), lambda i: (i, 0, 0)),
            whole((128 * 24, N)),
            matrix, matrix, matrix, matrix, matrix,
            whole((1, 128)),
        ],
        out_specs=pl.BlockSpec((16, 1, 48, 128), lambda i: (0, i, 0, 0)),
        scratch_shapes=SCRATCH,
        compiler_params=PARAMS,
        name="end_attention",
    )(columns, ends_mask, end_bias, *prepared(w_proj[1], w_out[1]), ln_gain[1:2])
    returned = lax.all_to_all(second, ROW, split_axis=0, concat_axis=0, tiled=True)
    return jnp.transpose(returned, (2, 0, 1, 3)).reshape(48, 96, 128)


def solution(mesh):
    parts = Mesh(mesh.devices.reshape(4, 2, 2, 4, 2), ("z", "x_hi", "core", "y", "x_lo"))
    return jax.shard_map(
        local,
        mesh=parts,
        in_specs=(P(ROW, COL, None), P(ROW, COL), P(), P(), P(), P(), P(), P()),
        out_specs=P(ROW, COL, None),
        check_vma=False,
    )
```

time: 1270 us -> 322 us (0.25)
  waiting for transfers between devices: 652 us -> 120 us
  matrix products: 258 us -> 6.43 us
  local copies, waits for them, and re-layouts: 172 us -> 17.6 us
  Pallas kernels: 0 us -> 75.3 us
  other arithmetic: 79.7 us -> 17.8 us
  starting transfers between devices: 26.9 us -> 9.37 us
  blocking collectives: 46.7 us -> 61.2 us
    all_gather x2, waiting for transfers between devices: 548 us -> 74.3 us  [the longest x1 43.2 us: local(): end_bias = lax.all_gather(end_shard, GATHER, axis=0, tiled=True)]
    dot_general x50 -> x1, matrix products: 258 us -> 6.43 us  [local(): jnp.einsum('jkc,ch->hjk', normed, w_bias[0], precision=lax.Precision.HIGH...]
    dynamic_update_slice x12 -> x0, local copies, waits for them, and re-layouts: 119 us -> none  [local(): lax.map(lambda inputs: attend(inputs[0], inputs[1], start_plane, w_proj[0...]
    pallas_call x0 -> x2, Pallas kernels: none -> 75.3 us  [the longest x1 40 us: local(): pl.pallas_call(start_kernel, grid=(LINES,), out_shape=(jax.ShapeDtypeStru...]
    all_to_all x5 -> x2, waiting for transfers between devices: 104 us -> 45.4 us  [the longest x1 27.8 us: local(): lax.all_to_all(first_pair.reshape(128, SLOT, 128), EVERY, split_axis=0, c...]
    mul x34 -> x0, other arithmetic: 22.9 us -> none  [the longest x4 11.9 us: layer_norm(): return centred * lax.rsqrt(variance + 1e-05) * scales]
    add x3 -> x0, other arithmetic: 20.7 us -> none  [the longest x1 11.2 us: local(): start_plane = start_plane + chain_gain[0][:, None, None] * same_chain[None]]
    all_to_all x5 -> x2, starting transfers between devices: 26.8 us -> 9.15 us  [the longest x1 5.4 us: local(): lax.all_to_all(first_pair.reshape(128, SLOT, 128), EVERY, split_axis=0, c...]
  transfers between devices with their start and end apart: 7 -> 4, of which waited for: 6 -> 4; matrix products, arithmetic and copies ran while one was open for 2% -> 7% of each run, Pallas kernels for 0% -> 0%
where the time goes in v1:
time: 322 us; the launch traced here: 321 us
  waiting for transfers between devices  120 us (37%)
  Pallas kernels  75.3 us (23%)
  blocking collectives  61.2 us (19%)
  other arithmetic  17.8 us (6%)
  local copies, waits for them, and re-layouts  17.6 us (5%)
  between operations  13.6 us (4%)
  starting transfers between devices  9.37 us (3%)
  matrix products  6.43 us (2%)
    all_gather x1, waiting for transfers between devices, local(): end_bias = lax.all_gather(end_shard, GATHER, axis=0, tiled=True)  43.2 us
    pallas_call x1, Pallas kernels, local(): pl.pallas_call(start_kernel, grid=(LINES,), out_shape=(jax.ShapeDtypeStru...  40 us
    all_to_all x1, blocking collectives, local(): lax.all_to_all(second, ROW, split_axis=0, concat_axis=0, tiled=True)  35.6 us
    pallas_call x1, Pallas kernels, local(): pl.pallas_call(end_kernel, grid=(LINES,), out_shape=jax.ShapeDtypeStruct(...  35.3 us
    all_gather x1, waiting for transfers between devices, local(): lax.all_gather(planes[:4].reshape(24, N), GATHER, axis=0, tiled=True)  31.1 us
    all_to_all x1, waiting for transfers between devices, local(): lax.all_to_all(first_pair.reshape(128, SLOT, 128), EVERY, split_axis=0, c...  27.8 us
    all_to_all x1, waiting for transfers between devices, local(): lax.all_to_all(pair_state, COL, split_axis=0, concat_axis=0, tiled=True)  17.5 us
    all_to_all x1, blocking collectives, local(): lax.all_to_all(planes, ROW, split_axis=0, concat_axis=0, tiled=True)  16.4 us
  transfers between devices with their start and end apart: 4, of which 4 were waited for; matrix products, arithmetic and copies ran while one was open for 7% of the time, Pallas kernels for 0%

profile of v1, /device:TPU:1, one launch (start us, length us, event | category | flops | bytes accessed | tf_op | source)
XLA Modules:
  0.0 321.0 jit_solution(17293739318911192798)
XLA Ops:
  6.5 0.8 dynamic_slice.9
  7.3 0.8 dynamic_slice.10
  8.1 1.3 fusion.23
  9.3 2.6 reduce_sum.18
  11.9 2.9 multiply_reduce_fusion
  15.0 6.4 %fusion.13 = f32[4,48,96]{2,0,1:T(4,128)S(1)} fusion(f32[48,96,128]{2,1,0:T(8,128)} %param.8, f32[128]{0:T(128)S(1)} %get-tuple-element.34, f32[48,96]{1,0:T(8,128)S(1)} %add_rsqrt_fusion, f32[48,96]{1,0:T(8,128)S(1)} %broadcast_multiply_fusion, f32[48,96]{1,0:T(8,128)S(1)} %compare_convert_fusion.1, f32[4]{0:T(128)S(1)} %get-tuple-element.32, ...), kind=kOutput, calls=%fused_computation.10 | convolution fusion | flops 30136320 | bytes 2509824 | tf_op jit(solution)/shard_map/jkc,ch->hjk/dot_general | solution.py:208
  22.1 16.4 %all_to_all.29 = f32[16,1,1440]{2,1,0:T(1,128)S(1)} all-to-all(f32[16,1,1440]{2,1,0:T(1,128)S(1)} %reshape.125), channel_id=1, replica_groups=mesh['z'=4,'x_hi'=2,'core'=2,'y'=4,'x_lo'=2] {'z','x_hi','core'}, dimensions={0} | all-to-all | bytes 184320 | tf_op jit(solution)/shard_map/all_to_all | solution.py:215
  39.0 0.9 reduce
  40.2 0.8 reshape.119
  41.0 9.1 %all_to_all.30 = f32[8,6,96]{2,1,0:T(8,128)S(1)} all-to-all(f32[8,6,96]{2,1,0:T(8,128)S(1)} %all_to_all.19), channel_id=1, replica_groups=mesh['z'=4,'x_hi'=2,'core'=2,'y'=4,'x_lo'=2] {'y','x_lo'}, dimensions={0} | all-to-all | bytes 36864 | tf_op jit(solution)/shard_map/all_to_all | solution.py:204
  50.1 3.7 %all-to-all-start = ((f32[48,96,128]{2,1,0:T(8,128)}), f32[48,96,128]{2,1,0:T(8,128)S(1)}, u32[]{:S(2)}, u32[]{:S(2)}) async-start(f32[48,96,128]{2,1,0:T(8,128)} %param.8), calls=%async_computation | async-start | bytes 4718592 | tf_op jit(solution)/shard_map/all_to_all | solution.py:202
  54.1 1.1 fusion.22
  55.4 0.7 slice_reduce-precision_fusion.3
  56.1 0.8 copy.38.w_key
  57.5 1.5 bitcast_reduce-precision_fusion
  59.0 0.8 maximum_convert_fusion
  61.2 0.7 maximum_bitcast_fusion.3.w_gate
  62.5 0.7 compare_convert_fusion.same
  63.2 3.7 %reshape.124.mask_ref = f32[6,768,1]{2,1,0:T(8,128)} reshape(f32[6,8,96]{2,1,0:T(8,128)S(1)} %copy.30) | data formatting | bytes 36864 | tf_op jit(solution)/shard_map/reshape | solution.py:205
  66.9 17.5 %all-to-all-done = f32[48,96,128]{2,1,0:T(8,128)S(1)} async-done(((f32[48,96,128]{2,1,0:T(8,128)}), f32[48,96,128]{2,1,0:T(8,128)S(1)}, u32[]{:S(2)}, u32[]{:S(2)}) %all-to-all-start) | async-done | bytes 2359328 | tf_op jit(solution)/shard_map/all_to_all | solution.py:202
  84.5 31.1 %all-gather.3.cloned.1.call-done.gathered = f32[3072,768]{1,0:T(8,128)} async-done(((f32[24,768]{1,0:T(8,128)}), f32[3072,768]{1,0:T(8,128)}) %all-gather.3.cloned.1.call-update) | async-done | bytes 9437200 | tf_op jit(solution)/shard_map/all_gather | solution.py:218
  116.2 40.0 %start_attention.1 = (f32[5120,128]{1,0:T(8,128)}, f32[24,768]{1,0:T(8,128)}) custom-call(f32[8,6,96,128]{3,2,1,0:T(8,128)} %bitcast.64, f32[6,768,1]{2,1,0:T(8,128)} %reshape.124.mask_ref, f32[3072,768]{1,0:T(8,128)} %all-gather.3.cloned.1.call-done.gathered, bf16[256,256]{1,0:T(8,128)(2,1)} %maximum_bitcast_fusion.1.w_query, bf16[256,256]{1,0:T(8,128)(2,1)} %copy.38.w_key, ...), custom_call_target="tpu_custom_call" | custom-call | tf_op jit(solution)/shard_map/start_attention/pallas_call | solution.py:225
  156.2 5.4 %all-to-all-start.3 = ((f32[128,40,128]{2,1,0:T(8,128)}), f32[128,40,128]{2,1,0:T(8,128)S(1)}, u32[]{:S(2)}, u32[]{:S(2)}) async-start(f32[128,40,128]{2,1,0:T(8,128)} %bitcast.65), calls=%async_computation.3 | async-start | bytes 5242880 | tf_op jit(solution)/shard_map/all_to_all | solution.py:249
  162.4 0.8 copy.42.w_key
  163.2 0.8 maximum_convert_fusion.9
  164.0 0.8 maximum_convert_fusion.5
  167.4 2.6 reshape_squeeze.4.mask_ref
  170.0 27.8 %all-to-all-done.3 = f32[128,40,128]{2,1,0:T(8,128)S(1)} async-done(((f32[128,40,128]{2,1,0:T(8,128)}), f32[128,40,128]{2,1,0:T(8,128)S(1)}, u32[]{:S(2)}, u32[]{:S(2)}) %all-to-all-start.3) | async-done | bytes 2621472 | tf_op jit(solution)/shard_map/all_to_all | solution.py:249
  197.9 43.2 %all-gather.5.cloned.1.call-done.gathered = f32[3072,768]{1,0:T(8,128)} async-done(((f32[24,768]{1,0:T(8,128)}), f32[3072,768]{1,0:T(8,128)}) %all-gather.5.cloned.1.call-update) | async-done | bytes 9437200 | tf_op jit(solution)/shard_map/all_gather | solution.py:248
  241.1 35.3 %end_attention.1 = f32[16,6,48,128]{3,2,1,0:T(8,128)} custom-call(f32[5120,128]{1,0:T(8,128)} %bitcast.62, f32[6,768,1]{2,1,0:T(8,128)} %reshape_squeeze.4.mask_ref, f32[3072,768]{1,0:T(8,128)} %all-gather.5.cloned.1.call-done.gathered, bf16[256,256]{1,0:T(8,128)(2,1)} %maximum_bitcast_fusion.4.w_query, bf16[256,256]{1,0:T(8,128)(2,1)} %copy.42.w_key, ...), custom_call_target="tpu_custom_call" | custom-call | tf_op jit(solution)/shard_map/end_attention/pallas_call | solution.py:252
  276.4 35.6 %all_to_all.31 = f32[16,6,48,128]{3,2,1,0:T(8,128)S(1)} all-to-all(f32[16,6,48,128]{3,2,1,0:T(8,128)} %end_attention.1), channel_id=1, replica_groups=mesh['z'=4,'x_hi'=2,'core'=2,'y'=4,'x_lo'=2] {'z','x_hi','core'}, dimensions={0} | all-to-all | bytes 4718592 | tf_op jit(solution)/shard_map/all_to_all | solution.py:268
  312.0 2.1 copy.43
  (56 shorter events, 8.8 us)
Async XLA Ops:
  6.5 109.0 %all-gather.3.cloned.1.call-start = ((), (), s32[]{:S(2)}) async-start(), calls=%async_computation.5 | async-start | bytes 9510912 | tf_op jit(solution)/shard_map/all_gather | solution.py:218
  9.3 5.5 %copy-start.5 = (f32[2,4]{1,0:T(2,128)S(1)}, f32[2,4]{1,0:T(2,128)}, u32[]{:S(2)}) copy-start(f32[2,4]{1,0:T(2,128)} %param.15) | copy-start | bytes 100
  9.3 5.6 %copy-start.4 = (f32[2,128,4]{1,2,0:T(4,128)S(1)}, f32[2,128,4]{1,2,0:T(4,128)}, u32[]{:S(2)}) copy-start(f32[2,128,4]{1,2,0:T(4,128)} %param.13) | copy-start | bytes 12292
  11.9 9.6 %copy-start.2 = (s32[48,96]{1,0:T(8,128)S(1)}, s32[48,96]{1,0:T(8,128)}, u32[]{:S(2)}) copy-start(s32[48,96]{1,0:T(8,128)} %param.9) | copy-start | bytes 55300
  50.1 5.1 %copy-start.3 = (s32[768]{0:T(1024)S(1)}, s32[768]{0:T(1024)}, u32[]{:S(2)}) copy-start(s32[768]{0:T(1024)} %param.10) | copy-start | bytes 9220
  50.1 34.3 %all-to-all-start = ((f32[48,96,128]{2,1,0:T(8,128)}), f32[48,96,128]{2,1,0:T(8,128)S(1)}, u32[]{:S(2)}, u32[]{:S(2)}) async-start(f32[48,96,128]{2,1,0:T(8,128)} %param.8), calls=%async_computation | async-start | bytes 4718592 | tf_op jit(solution)/shard_map/all_to_all | solution.py:202
  53.9 187.2 %all-gather.5.cloned.1.call-start = ((), (), s32[]{:S(2)}) async-start(), calls=%async_computation.6 | async-start | bytes 9510912 | tf_op jit(solution)/shard_map/all_gather | solution.py:248
  84.5 31.7 %copy-start.1 = (f32[48,96,128]{2,1,0:T(8,128)}, f32[48,96,128]{2,1,0:T(8,128)S(1)}, u32[]{:S(2)}) copy-start(f32[48,96,128]{2,1,0:T(8,128)S(1)} %all-to-all-done) | copy-start | bytes 7077892
  156.2 41.7 %all-to-all-start.3 = ((f32[128,40,128]{2,1,0:T(8,128)}), f32[128,40,128]{2,1,0:T(8,128)S(1)}, u32[]{:S(2)}, u32[]{:S(2)}) async-start(f32[128,40,128]{2,1,0:T(8,128)} %bitcast.65), calls=%async_computation.3 | async-start | bytes 5242880 | tf_op jit(solution)/shard_map/all_to_all | solution.py:249
  197.9 43.2 %copy-start = (f32[128,40,128]{2,1,0:T(8,128)}, f32[128,40,128]{2,1,0:T(8,128)S(1)}, u32[]{:S(2)}) copy-start(f32[128,40,128]{2,1,0:T(8,128)S(1)} %all-to-all-done.3) | copy-start | bytes 7864324
Sparse Core Ops, SparseCore 0:
  41.1 74.3 all-gather.2
  156.3 84.7 all-gather.4

commit v2 on v1

v2 whole, which is shorter than its diff:
```python
import functools
import jax
import jax.numpy as jnp
from jax import lax
from jax.experimental import pallas as pl
from jax.experimental.pallas import tpu as pltpu
from jax.sharding import Mesh, PartitionSpec as P

N = 768
HEADS = 4
LINES = 6
SLOT = 40
LOG2E = 1.4426950408889634
F32 = jnp.float32
BF16 = jnp.bfloat16
ROW = ("z", "x_hi", "core")
COL = ("y", "x_lo")
EVERY = ROW + COL
GATHER = ("z", "x_hi", "x_lo", "y", "core")
NT = (((1,), (1,)), ((), ()))
TN = (((0,), (0,)), ((), ()))


def split(values):
    high = values.astype(BF16)
    return high, (values - high.astype(F32)).astype(BF16)


def layer_norm(values, scales):
    average = jnp.mean(values, axis=-1, keepdims=True)
    centred = values - average
    variance = jnp.mean(centred * centred, axis=-1, keepdims=True)
    return centred * lax.rsqrt(variance + 1e-05) * scales


def halves(values):
    return values[:, :128] + values[:, 128:]


def gathered_place(row, col):
    return (row // 2) * 16 + (col % 2) * 8 + (col // 2) * 2 + row % 2


def order_tiles(gathered, bias):
    slot = lax.broadcasted_iota(jnp.int32, (1, 128), 1) // 16

    def step(col, _):
        for tile in range(6):
            pieces = []
            for t in range(8):
                row, part = divmod(tile * 8 + t, 3)
                start = pl.multiple_of(gathered_place(row, col) * 144 + part * 48, 8)
                pieces.append(gathered[pl.ds(start, 48), :])
            for distance in (4, 2, 1):
                upper = (slot // distance) % 2 == 1
                moved = list(pieces)
                for t in range(8):
                    if (t // distance) % 2 == 0:
                        one, two = pieces[t], pieces[t + distance]
                        moved[t] = jnp.where(upper, pltpu.roll(two, 16 * distance, 1), one)
                        moved[t + distance] = jnp.where(upper, two, pltpu.roll(one, 128 - 16 * distance, 1))
                pieces = moved
            for t in range(8):
                start = pl.multiple_of(col * 96 + (t // 4) * 48, 8)
                bias[t % 4, pl.ds(start, 48), tile * 128 : (tile + 1) * 128] = pieces[t]
        return 0

    lax.fori_loop(0, 8, step, 0)


def order_lines(gathered, bias):
    def step(outer, _):
        for part in range(4):
            owners = [gathered_place(outer * 2 + part // 2, (part % 2) * 4 + t) for t in range(4)]
            blocks = [gathered[pl.ds(pl.multiple_of(owner * 24, 8), 24), :] for owner in owners]
            start = pl.multiple_of(outer * 96 + part * 24, 8)
            for head in range(HEADS):
                rows = [block[head * LINES : (head + 1) * LINES] for block in blocks]
                bias[head, pl.ds(start, 24), :] = jnp.concatenate(rows, axis=0)
        return 0

    lax.fori_loop(0, 8, step, 0)


def tile_kernel(pair_ref, gain, w_lanes, chain, out_ref, normed):
    normed[...] = layer_norm(pair_ref[...].reshape(48 * 96, 128), gain[...])
    lane = lax.broadcasted_iota(jnp.int32, (128, 128), 1)
    total = chain[...]
    for t in range(16):
        rows = []
        for part in range(3):
            start = (part * 16 + t) * 96
            rows.append(jnp.concatenate([normed[start : start + 48, :], normed[start + 48 : start + 96, :]], axis=1))
        here = lane % 16 == t
        weights = jnp.concatenate(
            [jnp.where(here & (lane < 64), w_lanes[...], 0.0), jnp.where(here & (lane >= 64), w_lanes[...], 0.0)], axis=0
        )
        total = total + jnp.dot(
            jnp.concatenate(rows, axis=0), weights, precision=lax.Precision.HIGHEST, preferred_element_type=F32
        )
    out_ref[...] = total


def project(x, mask, w_query, w_key, w_value, w_gate, gain, query, key, value, gate):
    normed_high, normed_low = split(layer_norm(x, gain))
    normed = jnp.concatenate([normed_high, normed_low], axis=1)

    def turned(weights):
        both = lax.dot_general(weights[...], normed, NT, preferred_element_type=F32)
        return both[:128] + both[128:]

    key_proj = halves(jnp.dot(normed, w_key[...], preferred_element_type=F32))
    query_high, query_low = split(turned(w_query))
    value_high, value_low = split(turned(w_value))
    gate[0] = jax.nn.sigmoid(turned(w_gate))
    block = lax.broadcasted_iota(jnp.int32, (1, 128), 1) // 32
    masked = jnp.broadcast_to(mask - 1.0, (N, 128))
    key_high = key_proj.astype(BF16).astype(F32)
    key_low = pltpu.roll(key_proj - key_high, 64, 1)
    key_again = pltpu.roll(key_high, 32, 1)
    place = lax.broadcasted_iota(jnp.int32, (32, N), 0)
    weight = jnp.where(
        place == 0, 1442840576.0, jnp.where(place == 1, -145408.0, jnp.where(place == 2, -128.0, 0.0))
    ).astype(BF16)
    ones = jnp.ones((16, N), BF16)
    for head in range(HEADS):
        at = [(head + t) % 4 for t in range(4)]
        part = slice(head * 32, (head + 1) * 32)
        key[0, head] = jnp.where(
            block == at[0],
            key_high,
            jnp.where(block == at[1], key_again, jnp.where(block == at[2], key_low, masked)),
        ).astype(BF16)
        rows = [None] * 4
        rows[at[0]] = query_high[part]
        rows[at[1]] = query_low[part]
        rows[at[2]] = query_high[part]
        rows[at[3]] = weight
        query[0, head] = jnp.concatenate(rows, axis=0)
        value[0, head] = jnp.concatenate([value_high[part], value_low[part], ones], axis=0)


def attend(query, key, value, gate, bias, w_out, mixed):
    width = 256
    for head in range(HEADS):
        for start in range(0, N, width):
            span = slice(start, start + width)
            scores = jnp.dot(key[0, head], query[0, head, :, span], preferred_element_type=F32)
            scores = scores + bias[head, :, span]
            weights = jnp.exp2(scores - jnp.max(scores, axis=0, keepdims=True))
            high, low = split(weights)
            total = jnp.dot(value[0, head], high, preferred_element_type=F32)
            total = total + jnp.dot(value[0, head], low, preferred_element_type=F32)
            mixed[head * 32 : (head + 1) * 32, span] = (total[:32] + total[32:64]) / total[64:65]
    gated_high, gated_low = split(gate[0] * mixed[...])
    gated = jnp.concatenate([gated_high, gated_low], axis=0)
    return halves(lax.dot_general(gated, w_out[...], TN, preferred_element_type=F32))


def start_project_kernel(x_ref, mask_ref, w_query, w_key, w_value, w_gate, gain, query, key, value, gate):
    x = x_ref[...].reshape(N, 128)
    project(x, mask_ref[0], w_query, w_key, w_value, w_gate, gain[...], query, key, value, gate)


def end_project_kernel(x_ref, mask_ref, w_query, w_key, w_value, w_gate, gain, query, key, value, gate, line_ref, line):
    step = pl.program_id(0)
    for t in range(LINES):
        for group in range(16):
            line[pl.ds(group * 8 * LINES + t, 8, stride=LINES), :] = x_ref[
                pl.ds(group * 8 * SLOT + t * LINES + step, 8, stride=SLOT), :
            ]
    x = line[...]
    line_ref[0] = x
    project(x, mask_ref[0], w_query, w_key, w_value, w_gate, gain[...], query, key, value, gate)


def start_kernel(
    x_ref, query, key, value, gate, gathered, w_out, end_gain, w_bias, chain, same, pair_ref, bias_ref, bias, mixed, line
):
    step = pl.program_id(0)

    @pl.when(step == 0)
    def _():
        order_tiles(gathered, bias)
        pair_ref[...] = jnp.zeros_like(pair_ref)

    first = x_ref[...].reshape(N, 128) + attend(query, key, value, gate, bias, w_out, mixed)
    line[...] = first
    for row in range(16):
        for t in range(LINES):
            pair_ref[pl.ds(row * 8 * SLOT + step * LINES + t, 8, stride=SLOT), :] = line[
                pl.ds(row * LINES + t, 8, stride=96), :
            ]
    normed = layer_norm(first, end_gain[...])
    plane = lax.dot_general(
        w_bias[...], normed, NT, precision=lax.Precision.HIGHEST, preferred_element_type=F32
    )
    plane = (plane + chain[:, :1] * same[0]) * LOG2E
    for head in range(HEADS):
        bias_ref[pl.ds(head * LINES + step, 1), :] = plane[head : head + 1]


def end_kernel(x_ref, query, key, value, gate, gathered, w_out, out_ref, bias, mixed):
    @pl.when(pl.program_id(0) == 0)
    def _():
        order_lines(gathered, bias)

    update = attend(query, key, value, gate, bias, w_out, mixed)
    out_ref[...] = (x_ref[0] + update).reshape(16, 1, 48, 128)


def whole(shape):
    return pl.BlockSpec(shape, lambda i: (0,) * len(shape), pipeline_mode=pl.Buffered(1))


def lines(*shape):
    return pl.BlockSpec((1, *shape), lambda i: (i,) + (0,) * len(shape))


MATRIX = whole((256, 256))
PROJECTED = [lines(HEADS, 128, N), lines(HEADS, N, 128), lines(HEADS, 80, N), lines(128, N)]
PROJECTED_SHAPES = [
    jax.ShapeDtypeStruct((LINES, HEADS, 128, N), BF16),
    jax.ShapeDtypeStruct((LINES, HEADS, N, 128), BF16),
    jax.ShapeDtypeStruct((LINES, HEADS, 80, N), BF16),
    jax.ShapeDtypeStruct((LINES, 128, N), F32),
]
PARAMS = pltpu.CompilerParams(vmem_limit_bytes=56 * 1024 * 1024)


def doubled(weights):
    high = lax.reduce_precision(weights, 8, 7)
    both = jnp.concatenate([high, weights - high], axis=1)
    return jnp.concatenate([both, both], axis=0).astype(BF16)


def prepared(w_proj, w_out):
    w_query = doubled(w_proj[:, :128] * (32 ** -0.5 * LOG2E)).T
    w_key = doubled(w_proj[:, 128:256])
    w_value = doubled(w_proj[:, 256:384]).T
    w_gate = doubled(w_proj[:, 384:]).T
    return w_query, w_key, w_value, w_gate, doubled(w_out)


def local(pair_state, pair_mask, chain_ids, ln_gain, w_proj, w_bias, w_out, chain_gain):
    row, col = lax.axis_index(ROW), lax.axis_index(COL)
    mask_float = pair_mask.astype(F32)
    ids_row = lax.dynamic_slice(chain_ids, (row * 48,), (48,)).reshape(3, 1, 1, 1, 16)
    ids_col = lax.dynamic_slice(chain_ids, (col * 96,), (96,)).reshape(2, 48).T.reshape(1, 48, 2, 1, 1)
    same = (ids_row == ids_col).astype(F32)
    tile_chain = (same * (chain_gain[0] * LOG2E).reshape(1, 1, 1, 4, 1)).reshape(144, 128)
    w_lanes = jnp.tile(jnp.repeat(w_bias[0] * LOG2E, 16, axis=1), (1, 2))
    tile_bias = pl.pallas_call(
        tile_kernel,
        out_shape=jax.ShapeDtypeStruct((144, 128), F32),
        scratch_shapes=[pltpu.VMEM((48 * 96, 128), F32)],
        compiler_params=PARAMS,
        name="tile_bias",
    )(pair_state, ln_gain[0:1], w_lanes, tile_chain)
    start_bias = lax.all_gather(tile_bias, GATHER, axis=0, tiled=True)

    rows_pair = lax.all_to_all(pair_state, COL, split_axis=0, concat_axis=0, tiled=True)
    rows_pair = rows_pair.reshape(8, LINES, 96, 128)
    rows_mask = lax.all_to_all(mask_float, COL, split_axis=0, concat_axis=0, tiled=True)
    rows_mask = jnp.transpose(rows_mask.reshape(8, LINES, 96), (1, 0, 2)).reshape(LINES, N, 1)
    ends_mask = jnp.transpose(mask_float.reshape(48, 16, LINES), (1, 2, 0))
    ends_mask = lax.all_to_all(ends_mask, ROW, split_axis=0, concat_axis=0, tiled=True)
    ends_mask = jnp.transpose(ends_mask, (1, 0, 2)).reshape(LINES, N, 1)

    *start_weights, start_out = prepared(w_proj[0], w_out[0])
    *end_weights, end_out = prepared(w_proj[1], w_out[1])
    row_block = pl.BlockSpec((8, 1, 96, 128), lambda i: (0, i, 0, 0))
    start_parts = pl.pallas_call(
        start_project_kernel,
        grid=(LINES,),
        out_shape=PROJECTED_SHAPES,
        in_specs=[row_block, lines(N, 1), MATRIX, MATRIX, MATRIX, MATRIX, whole((1, 128))],
        out_specs=PROJECTED,
        compiler_params=PARAMS,
        name="start_projections",
    )(rows_pair, rows_mask, *start_weights, ln_gain[0:1])

    ids_line = lax.dynamic_slice(chain_ids, (row * 48 + col * LINES,), (LINES,))
    same_line = (ids_line[:, None] == chain_ids[None, :]).astype(F32).reshape(LINES, 1, N)
    end_w = jnp.concatenate([w_bias[1].T, jnp.zeros((4, 128), F32)], axis=0)
    chain = jnp.broadcast_to(jnp.concatenate([chain_gain[1], jnp.zeros((4,), F32)])[:, None], (8, 128))
    first_pair, end_shard = pl.pallas_call(
        start_kernel,
        grid=(LINES,),
        out_shape=(
            jax.ShapeDtypeStruct((128 * SLOT, 128), F32),
            jax.ShapeDtypeStruct((HEADS * LINES, N), F32),
        ),
        in_specs=[
            row_block, *PROJECTED, whole((128 * 144, 128)), MATRIX,
            whole((1, 128)), whole((8, 128)), whole((8, 128)), lines(1, N),
        ],
        out_specs=(whole((128 * SLOT, 128)), whole((HEADS * LINES, N))),
        scratch_shapes=[pltpu.VMEM((HEADS, N, N), F32), pltpu.VMEM((128, N), F32), pltpu.VMEM((N, 128), F32)],
        compiler_params=PARAMS,
        name="start_attention",
    )(rows_pair, *start_parts, start_bias, start_out, ln_gain[1:2], end_w, chain, same_line)

    end_bias = lax.all_gather(end_shard, GATHER, axis=0, tiled=True)
    columns = lax.all_to_all(
        first_pair.reshape(128, SLOT, 128), EVERY, split_axis=0, concat_axis=0, tiled=True
    ).reshape(128 * SLOT, 128)
    *end_parts, end_lines = pl.pallas_call(
        end_project_kernel,
        grid=(LINES,),
        out_shape=PROJECTED_SHAPES + [jax.ShapeDtypeStruct((LINES, N, 128), F32)],
        in_specs=[whole((128 * SLOT, 128)), lines(N, 1), MATRIX, MATRIX, MATRIX, MATRIX, whole((1, 128))],
        out_specs=PROJECTED + [lines(N, 128)],
        scratch_shapes=[pltpu.VMEM((N, 128), F32)],
        compiler_params=PARAMS,
        name="end_projections",
    )(columns, ends_mask, *end_weights, ln_gain[1:2])
    second = pl.pallas_call(
        end_kernel,
        grid=(LINES,),
        out_shape=jax.ShapeDtypeStruct((16, LINES, 48, 128), F32),
        in_specs=[lines(N, 128), *PROJECTED, whole((128 * 24, N)), MATRIX],
        out_specs=pl.BlockSpec((16, 1, 48, 128), lambda i: (0, i, 0, 0)),
        scratch_shapes=[pltpu.VMEM((HEADS, N, N), F32), pltpu.VMEM((128, N), F32)],
        compiler_params=PARAMS,
        name="end_attention",
    )(end_lines, *end_parts, end_bias, end_out)
    returned = lax.all_to_all(second, ROW, split_axis=0, concat_axis=0, tiled=True)
    return jnp.transpose(returned, (2, 0, 1, 3)).reshape(48, 96, 128)


def solution(mesh):
    parts = Mesh(mesh.devices.reshape(4, 2, 2, 4, 2), ("z", "x_hi", "core", "y", "x_lo"))
    return jax.shard_map(
        local,
        mesh=parts,
        in_specs=(P(ROW, COL, None), P(ROW, COL), P(), P(), P(), P(), P(), P()),
        out_specs=P(ROW, COL, None),
        check_vma=False,
    )
```

time: 322 us -> 311 us (0.966)
  Pallas kernels: 75.3 us -> 106 us
  waiting for transfers between devices: 120 us -> 94.8 us
  other arithmetic: 17.8 us -> 9.09 us
  matrix products: 6.43 us -> 0 us
    pallas_call x0 -> x3, Pallas kernels: none -> 26.2 us  [the longest x1 10.7 us: local(): pl.pallas_call(end_project_kernel, grid=(LINES,), out_shape=PROJECTED_SHA...]
    all_gather x1, waiting for transfers between devices: 43.2 us -> 20.1 us  [local(): end_bias = lax.all_gather(end_shard, GATHER, axis=0, tiled=True)]
    pallas_call x1, Pallas kernels: 40 us -> 47.4 us  [local(): pl.pallas_call(start_kernel, grid=(LINES,), out_shape=(jax.ShapeDtypeStru...]
    dot_general x1 -> x0, matrix products: 6.43 us -> none  [local(): jnp.einsum('jkc,ch->hjk', normed, w_bias[0], precision=lax.Precision.HIGH...]
    reduce_sum x2 -> x0, other arithmetic: 5.48 us -> none  [the longest x1 2.91 us: layer_norm(): variance = jnp.mean(centred * centred, axis=-1, keepdims=True)]
    all_to_all x1, blocking collectives: 16.4 us -> 11.6 us  [local(): lax.all_to_all(ends_mask, ROW, split_axis=0, concat_axis=0, tiled=True)]
    all_gather x1, waiting for transfers between devices: 31.1 us -> 27.3 us  [local(): start_bias = lax.all_gather(tile_bias, GATHER, axis=0, tiled=True)]
  transfers between devices with their start and end apart: 4 -> 4, of which waited for: 4 -> 4; matrix products, arithmetic and copies ran while one was open for 7% -> 6% of each run, Pallas kernels for 0% -> 7%
where the time goes in v2:
time: 311 us; the launch traced here: 310 us
  Pallas kernels  106 us (34%)
  waiting for transfers between devices  94.8 us (30%)
  blocking collectives  58.1 us (19%)
  local copies, waits for them, and re-layouts  20.5 us (7%)
  between operations  13.6 us (4%)
  other arithmetic  9.09 us (3%)
  starting transfers between devices  7.83 us (3%)
    pallas_call x1, Pallas kernels, local(): pl.pallas_call(start_kernel, grid=(LINES,), out_shape=(jax.ShapeDtypeStru...  47.4 us
    all_to_all x1, blocking collectives, local(): lax.all_to_all(second, ROW, split_axis=0, concat_axis=0, tiled=True)  35.7 us
    pallas_call x1, Pallas kernels, local(): pl.pallas_call(end_kernel, grid=(LINES,), out_shape=jax.ShapeDtypeStruct(...  32.9 us
    all_to_all x1, waiting for transfers between devices, local(): lax.all_to_all(first_pair.reshape(128, SLOT, 128), EVERY, split_axis=0, c...  29.2 us
    all_gather x1, waiting for transfers between devices, local(): start_bias = lax.all_gather(tile_bias, GATHER, axis=0, tiled=True)  27.3 us
    all_gather x1, waiting for transfers between devices, local(): end_bias = lax.all_gather(end_shard, GATHER, axis=0, tiled=True)  20.1 us
    all_to_all x1, waiting for transfers between devices, local(): lax.all_to_all(pair_state, COL, split_axis=0, concat_axis=0, tiled=True)  18.2 us
    all_to_all x1, blocking collectives, local(): lax.all_to_all(ends_mask, ROW, split_axis=0, concat_axis=0, tiled=True)  11.6 us
  transfers between devices with their start and end apart: 4, of which 4 were waited for; matrix products, arithmetic and copies ran while one was open for 6% of the time, Pallas kernels for 7%

profile of v2, /device:TPU:1, one launch (start us, length us, event | category | flops | bytes accessed | tf_op | source)
XLA Modules:
  0.0 310.5 jit_solution(2456699324330069118)
XLA Ops:
  6.5 1.3 fusion.5
  7.8 0.8 dynamic_slice.9
  8.7 0.8 dynamic_slice.10
  10.0 0.8 slice_bitcast_fusion.1
  10.9 0.7 slice_bitcast_fusion
  11.6 0.7 copy.24.w_lanes
  13.0 5.0 %tile_bias.1 = f32[144,128]{1,0:T(8,128)} custom-call(f32[48,96,128]{2,1,0:T(8,128)} %pair_ref.1, f32[1,128]{1,0:T(1,128)} %get-tuple-element.54.gain, f32[128,128]{1,0:T(8,128)} %copy.24.w_lanes, f32[144,128]{1,0:T(8,128)} %broadcast_multiply_fusion.chain), custom_call_target="tpu_custom_call" | custom-call | tf_op jit(solution)/shard_map/tile_bias/pallas_call | solution.py:253
  18.0 10.9 %all_to_all.29 = f32[8,6,96]{2,1,0:T(8,128)S(1)} all-to-all(f32[8,6,96]{2,1,0:T(8,128)S(1)} %all_to_all.19), channel_id=1, replica_groups=mesh['z'=4,'x_hi'=2,'core'=2,'y'=4,'x_lo'=2] {'y','x_lo'}, dimensions={0} | all-to-all | bytes 36864 | tf_op jit(solution)/shard_map/all_to_all | solution.py:264
  28.9 3.8 %all-to-all-start = ((f32[48,96,128]{2,1,0:T(8,128)}), f32[48,96,128]{2,1,0:T(8,128)S(1)}, u32[]{:S(2)}, u32[]{:S(2)}) async-start(f32[48,96,128]{2,1,0:T(8,128)} %pair_ref.1), calls=%async_computation | async-start | bytes 4718592 | tf_op jit(solution)/shard_map/all_to_all | solution.py:262
  32.9 1.1 fusion.4
  34.2 0.7 copy.21.w_key
  35.7 0.7 maximum_bitcast_fusion.w_query
  38.4 0.7 compare_convert_fusion.same
  39.1 3.7 %reshape.110.mask_ref = f32[6,768,1]{2,1,0:T(8,128)} reshape(f32[6,8,96]{2,1,0:T(8,128)S(1)} %copy.18) | data formatting | bytes 36864 | tf_op jit(solution)/shard_map/reshape | solution.py:265
  42.8 18.2 %all-to-all-done = f32[48,96,128]{2,1,0:T(8,128)S(1)} async-done(((f32[48,96,128]{2,1,0:T(8,128)}), f32[48,96,128]{2,1,0:T(8,128)S(1)}, u32[]{:S(2)}, u32[]{:S(2)}) %all-to-all-start) | async-done | bytes 2359328 | tf_op jit(solution)/shard_map/all_to_all | solution.py:262
  61.0 1.4 copy-done
  62.4 10.5 %start_projections.1 = (bf16[6,4,128,768]{3,2,1,0:T(8,128)(2,1)}, bf16[6,4,768,128]{3,2,1,0:T(8,128)(2,1)}, bf16[6,4,80,768]{3,2,1,0:T(8,128)(2,1)}, f32[6,128,768]{2,1,0:T(8,128)}) custom-call(f32[8,6,96,128]{3,2,1,0:T(8,128)} %bitcast.50, f32[6,768,1]{2,1,0:T(8,128)} %reshape.110.mask_ref, bf16[256,256]{1,0:T(8,128)(2,1)} %maximum_bitcast_fusion.w_query, ...), custom_call_target="tpu_custom_call" | custom-call | tf_op jit(solution)/shard_map/start_projections/pallas_call | solution.py:273
  72.8 27.3 %all-gather.3.cloned.1.call-done.gathered = f32[18432,128]{1,0:T(8,128)} async-done(((f32[144,128]{1,0:T(8,128)}), f32[18432,128]{1,0:T(8,128)}) %all-gather.3.cloned.1.call-update) | async-done | bytes 9437200 | tf_op jit(solution)/shard_map/all_gather | solution.py:260
  100.8 47.4 %start_attention.1 = (f32[5120,128]{1,0:T(8,128)}, f32[24,768]{1,0:T(8,128)}) custom-call(f32[8,6,96,128]{3,2,1,0:T(8,128)} %bitcast.51, bf16[6,4,128,768]{3,2,1,0:T(8,128)(2,1)} %get-tuple-element.16.query, bf16[6,4,768,128]{3,2,1,0:T(8,128)(2,1)} %get-tuple-element.17.key, bf16[6,4,80,768]{3,2,1,0:T(8,128)(2,1)} %get-tuple-element.18.value, ...), custom_call_target="tpu_custom_call" | custom-call | tf_op jit(solution)/shard_map/start_attention/pallas_call | solution.py:287
  148.4 11.6 %all_to_all.30 = f32[16,1,288]{2,1,0:T(1,128)S(1)} all-to-all(f32[16,1,288]{2,1,0:T(1,128)S(1)} %reshape.112), channel_id=1, replica_groups=mesh['z'=4,'x_hi'=2,'core'=2,'y'=4,'x_lo'=2] {'z','x_hi','core'}, dimensions={0} | all-to-all | bytes 36864 | tf_op jit(solution)/shard_map/all_to_all | solution.py:267
  160.0 3.9 %all-to-all-start.2 = ((f32[128,40,128]{2,1,0:T(8,128)}), f32[128,40,128]{2,1,0:T(8,128)S(1)}, u32[]{:S(2)}, u32[]{:S(2)}) async-start(f32[128,40,128]{2,1,0:T(8,128)} %bitcast.54), calls=%async_computation.2 | async-start | bytes 5242880 | tf_op jit(solution)/shard_map/all_to_all | solution.py:305
  164.1 0.8 copy.29.w_key
  166.2 0.7 maximum_bitcast_fusion.5.w_gate
  168.1 0.7 reduce
  168.9 2.6 reshape.111.mask_ref
  171.5 29.2 %all-to-all-done.2 = f32[128,40,128]{2,1,0:T(8,128)S(1)} async-done(((f32[128,40,128]{2,1,0:T(8,128)}), f32[128,40,128]{2,1,0:T(8,128)S(1)}, u32[]{:S(2)}, u32[]{:S(2)}) %all-to-all-start.2) | async-done | bytes 2621472 | tf_op jit(solution)/shard_map/all_to_all | solution.py:305
  200.7 1.5 copy-done.1
  202.2 10.7 %end_projections.1 = (bf16[6,4,128,768]{3,2,1,0:T(8,128)(2,1)}, bf16[6,4,768,128]{3,2,1,0:T(8,128)(2,1)}, bf16[6,4,80,768]{3,2,1,0:T(8,128)(2,1)}, f32[6,128,768]{2,1,0:T(8,128)}, f32[6,768,128]{2,1,0:T(8,128)}) custom-call(f32[5120,128]{1,0:T(8,128)} %bitcast.52, f32[6,768,1]{2,1,0:T(8,128)} %reshape.111.mask_ref, ...), custom_call_target="tpu_custom_call" | custom-call | tf_op jit(solution)/shard_map/end_projections/pallas_call | solution.py:308
  212.9 20.1 %all-gather.5.cloned.1.call-done.gathered = f32[3072,768]{1,0:T(8,128)} async-done(((f32[24,768]{1,0:T(8,128)}), f32[3072,768]{1,0:T(8,128)}) %all-gather.5.cloned.1.call-update) | async-done | bytes 9437200 | tf_op jit(solution)/shard_map/all_gather | solution.py:304
  233.0 32.9 %end_attention.1 = f32[16,6,48,128]{3,2,1,0:T(8,128)} custom-call(f32[6,768,128]{2,1,0:T(8,128)} %get-tuple-element.21.x_ref, bf16[6,4,128,768]{3,2,1,0:T(8,128)(2,1)} %get-tuple-element.22.query, bf16[6,4,768,128]{3,2,1,0:T(8,128)(2,1)} %get-tuple-element.23.key, bf16[6,4,80,768]{3,2,1,0:T(8,128)(2,1)} %get-tuple-element.24.value, ...), custom_call_target="tpu_custom_call" | custom-call | tf_op jit(solution)/shard_map/end_attention/pallas_call | solution.py:318
  265.8 35.7 %all_to_all.31 = f32[16,6,48,128]{3,2,1,0:T(8,128)S(1)} all-to-all(f32[16,6,48,128]{3,2,1,0:T(8,128)} %end_attention.1), channel_id=1, replica_groups=mesh['z'=4,'x_hi'=2,'core'=2,'y'=4,'x_lo'=2] {'z','x_hi','core'}, dimensions={0} | all-to-all | bytes 4718592 | tf_op jit(solution)/shard_map/all_to_all | solution.py:328
  301.5 2.1 copy.30
  (58 shorter events, 8.2 us)
Async XLA Ops:
  6.5 11.5 %copy-start.3 = (s32[48,96]{1,0:T(8,128)S(1)}, s32[48,96]{1,0:T(8,128)}, u32[]{:S(2)}) copy-start(s32[48,96]{1,0:T(8,128)} %param.9) | copy-start | bytes 55300
  6.5 93.6 %all-gather.3.cloned.1.call-start = ((), (), s32[]{:S(2)}) async-start(), calls=%async_computation.5 | async-start | bytes 9510912 | tf_op jit(solution)/shard_map/all_gather | solution.py:260
  28.9 6.0 %copy-start.4 = (s32[768]{0:T(1024)S(1)}, s32[768]{0:T(1024)}, u32[]{:S(2)}) copy-start(s32[768]{0:T(1024)} %param.10) | copy-start | bytes 9220
  28.9 6.7 %copy-start.2 = (f32[2,128,128]{2,1,0:T(8,128)S(1)}, f32[2,128,128]{2,1,0:T(8,128)}, u32[]{:S(2)}) copy-start(f32[2,128,128]{2,1,0:T(8,128)} %param.14) | copy-start | bytes 393220
  28.9 32.1 %all-to-all-start = ((f32[48,96,128]{2,1,0:T(8,128)}), f32[48,96,128]{2,1,0:T(8,128)S(1)}, u32[]{:S(2)}, u32[]{:S(2)}) async-start(f32[48,96,128]{2,1,0:T(8,128)} %pair_ref.1), calls=%async_computation | async-start | bytes 4718592 | tf_op jit(solution)/shard_map/all_to_all | solution.py:262
  32.7 200.3 %all-gather.5.cloned.1.call-start = ((), (), s32[]{:S(2)}) async-start(), calls=%async_computation.6 | async-start | bytes 9510912 | tf_op jit(solution)/shard_map/all_gather | solution.py:304
  61.0 1.4 copy-start
  160.0 40.7 %all-to-all-start.2 = ((f32[128,40,128]{2,1,0:T(8,128)}), f32[128,40,128]{2,1,0:T(8,128)S(1)}, u32[]{:S(2)}, u32[]{:S(2)}) async-start(f32[128,40,128]{2,1,0:T(8,128)} %bitcast.54), calls=%async_computation.2 | async-start | bytes 5242880 | tf_op jit(solution)/shard_map/all_to_all | solution.py:305
  200.7 1.5 copy-start.1
Sparse Core Ops, SparseCore 0:
  18.1 81.9 all-gather.2
  148.3 84.5 all-gather.4

commit v3 on v2

v3 whole, which is shorter than its diff:
```python
import functools
import jax
import jax.numpy as jnp
from jax import lax
from jax.experimental import pallas as pl
from jax.experimental.pallas import tpu as pltpu
from jax.sharding import Mesh, PartitionSpec as P

N = 768
HEADS = 4
LINES = 6
SLOT = 40
PART = 584
PAIR = 1
LOG2E = 1.4426950408889634
F32 = jnp.float32
BF16 = jnp.bfloat16
ROW = ("z", "x_hi", "core")
COL = ("y", "x_lo")
EVERY = ROW + COL
NT = (((1,), (1,)), ((), ()))
TN = (((0,), (0,)), ((), ()))


def split(values):
    high = values.astype(BF16)
    return high, (values - high.astype(F32)).astype(BF16)


def layer_norm(values, scales):
    average = jnp.mean(values, axis=-1, keepdims=True)
    centred = values - average
    variance = jnp.mean(centred * centred, axis=-1, keepdims=True)
    return centred * lax.rsqrt(variance + 1e-05) * scales


def halves(values):
    return values[:, :128] + values[:, 128:]


def start_place(row, col):
    ahead = lax.rem(col // 2 + 4 - lax.axis_index("y"), 4)
    along_y = jnp.where(ahead == 0, 0, jnp.where(ahead == 1, 2, jnp.where(ahead == 2, 3, 1)))
    return ((row // 2 * 2 + col % 2) * 2 + row % 2) * 4 + along_y


def gather_start(shard):
    received = [lax.ppermute(shard, "y", [(t, (t + hop) % 4) for t in range(4)]) for hop in (1, 3, 2)]
    blocks = jnp.concatenate([shard, *received], axis=0)
    return lax.all_gather(blocks, ("z", "x_hi", "x_lo", "core"), axis=0, tiled=True)


def end_place(row, col):
    return (row // 2) * 16 + (col % 2) * 8 + (col // 2) * 2 + row % 2


def gather_end(shard):
    return lax.all_gather(shard, ("z", "x_hi", "x_lo", "y", "core"), axis=0, tiled=True)


def order_tiles(gathered, bias):
    slot = lax.broadcasted_iota(jnp.int32, (1, 128), 1) // 16

    def step(col, _):
        for tile in range(6):
            pieces = []
            for t in range(8):
                row, part = divmod(tile * 8 + t, 3)
                start = pl.multiple_of(start_place(row, col) * 144 + part * 48, 8)
                pieces.append(gathered[pl.ds(start, 48), :])
            for distance in (4, 2, 1):
                upper = (slot // distance) % 2 == 1
                moved = list(pieces)
                for t in range(8):
                    if (t // distance) % 2 == 0:
                        one, two = pieces[t], pieces[t + distance]
                        moved[t] = jnp.where(upper, pltpu.roll(two, 16 * distance, 1), one)
                        moved[t + distance] = jnp.where(upper, two, pltpu.roll(one, 128 - 16 * distance, 1))
                pieces = moved
            for t in range(8):
                start = pl.multiple_of(col * 96 + (t // 4) * 48, 8)
                bias[t % 4, pl.ds(start, 48), tile * 128 : (tile + 1) * 128] = pieces[t]
        return 0

    lax.fori_loop(0, 8, step, 0)


def order_lines(gathered, bias):
    def step(outer, _):
        for part in range(4):
            owners = [end_place(outer * 2 + part // 2, (part % 2) * 4 + t) for t in range(4)]
            blocks = [gathered[pl.ds(pl.multiple_of(owner * 24, 8), 24), :] for owner in owners]
            start = pl.multiple_of(outer * 96 + part * 24, 8)
            for head in range(HEADS):
                rows = [block[head * LINES : (head + 1) * LINES] for block in blocks]
                bias[head, pl.ds(start, 24), :] = jnp.concatenate(rows, axis=0)
        return 0

    lax.fori_loop(0, 8, step, 0)


def tile_kernel(ids, chain_gain, pair_ref, mask_ref, gain, w_bias, out_ref, parts_ref, normed):
    mask = jnp.concatenate([mask_ref[...].astype(F32), jnp.zeros((48, 32), F32)], axis=1)
    for part in range(8):
        inside = slice(part * LINES, (part + 1) * LINES)
        parts_ref[part, : LINES * 96] = pair_ref[inside].reshape(LINES * 96, 128)
        parts_ref[part, LINES * 96 :] = jnp.concatenate([mask[inside], jnp.zeros((2, 128), F32)], axis=0)
    normed[...] = layer_norm(pair_ref[...].reshape(48 * 96, 128), gain[:1])
    lane = lax.broadcasted_iota(jnp.int32, (128, 128), 1)
    head = (lane // 16) % 4
    w_lanes = sum(jnp.where(head == t, w_bias[0][:, t : t + 1] * LOG2E, 0.0) for t in range(HEADS))
    first_row, first_col = lax.axis_index(ROW) * 48, lax.axis_index(COL) * 96
    wide = lane[:1]
    gains = sum(jnp.where(head[:1] == t, chain_gain[0, t] * LOG2E, 0.0) for t in range(HEADS))
    place = lax.broadcasted_iota(jnp.int32, (48, 128), 0)
    keys = jnp.zeros((48, 128), jnp.int32)
    for t in range(48):
        ends = jnp.where(wide < 64, ids[first_col + t], ids[first_col + 48 + t])
        keys = jnp.where(place == t, ends, keys)
    total = []
    for part in range(3):
        queries = sum(jnp.where(wide % 16 == t, ids[first_row + part * 16 + t], 0) for t in range(16))
        total.append(jnp.where(keys == queries, gains, 0.0))
    total = jnp.concatenate(total, axis=0)
    for t in range(16):
        rows = []
        for part in range(3):
            start = (part * 16 + t) * 96
            rows.append(jnp.concatenate([normed[start : start + 48, :], normed[start + 48 : start + 96, :]], axis=1))
        here = lane % 16 == t
        weights = jnp.concatenate(
            [jnp.where(here & (lane < 64), w_lanes, 0.0), jnp.where(here & (lane >= 64), w_lanes, 0.0)], axis=0
        )
        total = total + jnp.dot(
            jnp.concatenate(rows, axis=0), weights, precision=lax.Precision.HIGHEST, preferred_element_type=F32
        )
    out_ref[...] = total


def project(x, mask, w_query, w_key, w_value, w_gate, gain, query, key, value, gate):
    normed_high, normed_low = split(layer_norm(x, gain))
    normed = jnp.concatenate([normed_high, normed_low], axis=1)

    def turned(weights):
        both = lax.dot_general(weights[...], normed, NT, preferred_element_type=F32)
        return both[:128] + both[128:]

    key_proj = halves(jnp.dot(normed, w_key[...], preferred_element_type=F32))
    query_high, query_low = split(turned(w_query))
    value_high, value_low = split(turned(w_value))
    gate[0] = jax.nn.sigmoid(turned(w_gate))
    block = lax.broadcasted_iota(jnp.int32, (1, 128), 1) // 32
    masked = jnp.broadcast_to(mask - 1.0, (N, 128))
    key_high = key_proj.astype(BF16).astype(F32)
    key_low = pltpu.roll(key_proj - key_high, 64, 1)
    key_again = pltpu.roll(key_high, 32, 1)
    place = lax.broadcasted_iota(jnp.int32, (32, N), 0)
    weight = jnp.where(
        place == 0, 1442840576.0, jnp.where(place == 1, -145408.0, jnp.where(place == 2, -128.0, 0.0))
    ).astype(BF16)
    ones = jnp.ones((16, N), BF16)
    for head in range(HEADS):
        at = [(head + t) % 4 for t in range(4)]
        part = slice(head * 32, (head + 1) * 32)
        key[0, head] = jnp.where(
            block == at[0],
            key_high,
            jnp.where(block == at[1], key_again, jnp.where(block == at[2], key_low, masked)),
        ).astype(BF16)
        rows = [None] * 4
        rows[at[0]] = query_high[part]
        rows[at[1]] = query_low[part]
        rows[at[2]] = query_high[part]
        rows[at[3]] = weight
        query[0, head] = jnp.concatenate(rows, axis=0)
        value[0, head] = jnp.concatenate([value_high[part], value_low[part], ones], axis=0)


def attend(t, query, key, value, gate, bias, w_out, mixed):
    width = 256
    for head in range(HEADS):
        for start in range(0, N, width):
            span = slice(start, start + width)
            scores = jnp.dot(key[t, head], query[t, head, :, span], preferred_element_type=F32)
            scores = scores + bias[head, :, span]
            weights = jnp.exp2(scores - jnp.max(scores, axis=0, keepdims=True))
            high, low = split(weights)
            total = jnp.dot(value[t, head], high, preferred_element_type=F32)
            total = total + jnp.dot(value[t, head], low, preferred_element_type=F32)
            mixed[t, head * 32 : (head + 1) * 32, span] = (total[:32] + total[32:64]) / total[64:65]
    gated_high, gated_low = split(gate[t] * mixed[t])
    gated = jnp.concatenate([gated_high, gated_low], axis=0)
    return halves(lax.dot_general(gated, w_out[...], TN, preferred_element_type=F32))


def start_project_kernel(x_ref, mask_ref, w_query, w_key, w_value, w_gate, gain, query, key, value, gate):
    x = x_ref[...].reshape(N, 128)
    held = mask_ref[:, pl.ds(pl.program_id(0), 1), :].reshape(8, 128).T
    mask = jnp.concatenate([held[:96, part : part + 1] for part in range(8)], axis=0)
    project(x, mask, w_query, w_key, w_value, w_gate, gain[...], query, key, value, gate)


def end_project_kernel(x_ref, w_query, w_key, w_value, w_gate, gain, query, key, value, gate, line_ref, line, mask):
    step = pl.program_id(0)
    lane = lax.broadcasted_iota(jnp.int32, (1, 128), 1)
    for group in range(16):
        held = x_ref[pl.ds(group * 8 * SLOT + LINES * LINES, 8, stride=SLOT), :]
        for t in range(LINES):
            place = pl.ds(group * 8 * LINES + t, 8, stride=LINES)
            line[place, :] = x_ref[pl.ds(group * 8 * SLOT + t * LINES + step, 8, stride=SLOT), :]
            own = jnp.sum(jnp.where(lane == t * LINES + step, held, 0.0), axis=1, keepdims=True)
            mask[place, :] = jnp.broadcast_to(own, (8, 128))
    x = line[...]
    line_ref[0] = x
    project(x, mask[...], w_query, w_key, w_value, w_gate, gain[...], query, key, value, gate)


def start_kernel(
    x_ref, mask_ref, query, key, value, gate, gathered, w_out, end_gain, w_bias, chain, same, pair_ref, bias_ref, bias, mixed, line
):
    step = pl.program_id(0)

    @pl.when(step == 0)
    def _():
        order_tiles(gathered, bias)
        pair_ref[...] = jnp.zeros_like(pair_ref)
        for group in range(16):
            pair_ref[pl.ds(group * 8 * SLOT + LINES * LINES, 8, stride=SLOT), :] = mask_ref[group * 8 : group * 8 + 8]

    for t in range(PAIR):
        first = x_ref[...].reshape(N, 128) + attend(t, query, key, value, gate, bias, w_out, mixed)
        line[t] = first
        here = step * PAIR + t
        for row in range(16):
            for k in range(LINES):
                pair_ref[pl.ds(row * 8 * SLOT + here * LINES + k, 8, stride=SLOT), :] = line[
                    t, pl.ds(row * LINES + k, 8, stride=96), :
                ]
        normed = layer_norm(first, end_gain[...])
        plane = lax.dot_general(
            w_bias[...], normed, NT, precision=lax.Precision.HIGHEST, preferred_element_type=F32
        )
        plane = (plane + chain[:, :1] * same[t]) * LOG2E
        for head in range(HEADS):
            bias_ref[pl.ds(head * LINES + here, 1), :] = plane[head : head + 1]


def end_kernel(x_ref, query, key, value, gate, gathered, w_out, out_ref, bias, mixed):
    @pl.when(pl.program_id(0) == 0)
    def _():
        order_lines(gathered, bias)

    for t in range(PAIR):
        update = attend(t, query, key, value, gate, bias, w_out, mixed)
        out_ref[:, t] = (x_ref[t] + update).reshape(16, 48, 128)


def whole(shape):
    return pl.BlockSpec(shape, lambda i: (0,) * len(shape), pipeline_mode=pl.Buffered(1))


def lines(*shape, count=1):
    return pl.BlockSpec((count, *shape), lambda i: (i,) + (0,) * len(shape))


def projected(count):
    shapes = [(HEADS, 128, N), (HEADS, N, 128), (HEADS, 80, N), (128, N)]
    return [lines(*shape, count=count) for shape in shapes]


MATRIX = whole((256, 256))
PROJECTED_SHAPES = [
    jax.ShapeDtypeStruct((LINES, HEADS, 128, N), BF16),
    jax.ShapeDtypeStruct((LINES, HEADS, N, 128), BF16),
    jax.ShapeDtypeStruct((LINES, HEADS, 80, N), BF16),
    jax.ShapeDtypeStruct((LINES, 128, N), F32),
]
PARAMS = pltpu.CompilerParams(vmem_limit_bytes=56 * 1024 * 1024)


def doubled(weights):
    high = lax.reduce_precision(weights, 8, 7)
    both = jnp.concatenate([high, weights - high], axis=1)
    return jnp.concatenate([both, both], axis=0).astype(BF16)


def prepared(w_proj, w_out):
    w_query = doubled(w_proj[:, :128] * (32 ** -0.5 * LOG2E)).T
    w_key = doubled(w_proj[:, 128:256])
    w_value = doubled(w_proj[:, 256:384]).T
    w_gate = doubled(w_proj[:, 384:]).T
    return w_query, w_key, w_value, w_gate, doubled(w_out)


def local(pair_state, pair_mask, chain_ids, ln_gain, w_proj, w_bias, w_out, chain_gain):
    row, col = lax.axis_index(ROW), lax.axis_index(COL)
    tile_bias, parts = pl.pallas_call(
        tile_kernel,
        out_shape=(jax.ShapeDtypeStruct((144, 128), F32), jax.ShapeDtypeStruct((8, PART, 128), F32)),
        in_specs=[
            pl.BlockSpec(memory_space=pltpu.SMEM),
            pl.BlockSpec(memory_space=pltpu.SMEM),
            pl.BlockSpec(memory_space=pltpu.VMEM),
            pl.BlockSpec(memory_space=pltpu.VMEM),
            pl.BlockSpec(memory_space=pltpu.VMEM),
            pl.BlockSpec(memory_space=pltpu.VMEM),
        ],
        scratch_shapes=[pltpu.VMEM((48 * 96, 128), F32)],
        compiler_params=PARAMS,
        name="tile_bias",
    )(chain_ids, chain_gain, pair_state, pair_mask, ln_gain, w_bias)
    start_bias = gather_start(tile_bias)

    rows = lax.all_to_all(parts, COL, split_axis=0, concat_axis=0, tiled=True)
    sent_mask = rows[:, LINES * 96 : LINES * 97, :96].reshape(8, LINES, 16, LINES)
    sent_mask = jnp.transpose(sent_mask, (2, 0, 1, 3)).reshape(128, LINES * LINES)
    sent_mask = jnp.pad(sent_mask, ((0, 0), (0, 128 - LINES * LINES)))

    *start_weights, start_out = prepared(w_proj[0], w_out[0])
    *end_weights, end_out = prepared(w_proj[1], w_out[1])
    row_block = pl.BlockSpec((8, 96, 128), lambda i: (0, i, 0))
    start_parts = pl.pallas_call(
        start_project_kernel,
        grid=(LINES,),
        out_shape=PROJECTED_SHAPES,
        in_specs=[row_block, pl.BlockSpec((8, 8, 128), lambda i: (0, 72, 0)), MATRIX, MATRIX, MATRIX, MATRIX, whole((1, 128))],
        out_specs=projected(1),
        compiler_params=PARAMS,
        name="start_projections",
    )(rows, rows, *start_weights, ln_gain[0:1])

    ids_line = lax.dynamic_slice(chain_ids, (row * 48 + col * LINES,), (LINES,))
    same_line = (ids_line[:, None] == chain_ids[None, :]).astype(F32).reshape(LINES, 1, N)
    end_w = jnp.concatenate([w_bias[1].T, jnp.zeros((4, 128), F32)], axis=0)
    chain = jnp.broadcast_to(jnp.concatenate([chain_gain[1], jnp.zeros((4,), F32)])[:, None], (8, 128))
    first_pair, end_shard = pl.pallas_call(
        start_kernel,
        grid=(LINES // PAIR,),
        out_shape=(
            jax.ShapeDtypeStruct((128 * SLOT, 128), F32),
            jax.ShapeDtypeStruct((HEADS * LINES, N), F32),
        ),
        in_specs=[
            row_block, whole((128, 128)),
            *projected(PAIR), whole((128 * 144, 128)), MATRIX,
            whole((1, 128)), whole((8, 128)), whole((8, 128)), lines(1, N, count=PAIR),
        ],
        out_specs=(whole((128 * SLOT, 128)), whole((HEADS * LINES, N))),
        scratch_shapes=[
            pltpu.VMEM((HEADS, N, N), F32),
            pltpu.VMEM((PAIR, 128, N), F32),
            pltpu.VMEM((PAIR, N, 128), F32),
        ],
        compiler_params=PARAMS,
        name="start_attention",
    )(rows, sent_mask, *start_parts, start_bias, start_out, ln_gain[1:2], end_w, chain, same_line)

    end_bias = gather_end(end_shard)
    columns = lax.all_to_all(
        first_pair.reshape(128, SLOT, 128), EVERY, split_axis=0, concat_axis=0, tiled=True
    ).reshape(128 * SLOT, 128)
    *end_parts, end_lines = pl.pallas_call(
        end_project_kernel,
        grid=(LINES,),
        out_shape=PROJECTED_SHAPES + [jax.ShapeDtypeStruct((LINES, N, 128), F32)],
        in_specs=[whole((128 * SLOT, 128)), MATRIX, MATRIX, MATRIX, MATRIX, whole((1, 128))],
        out_specs=projected(1) + [lines(N, 128)],
        scratch_shapes=[pltpu.VMEM((N, 128), F32), pltpu.VMEM((N, 128), F32)],
        compiler_params=PARAMS,
        name="end_projections",
    )(columns, *end_weights, ln_gain[1:2])
    second = pl.pallas_call(
        end_kernel,
        grid=(LINES // PAIR,),
        out_shape=jax.ShapeDtypeStruct((16, LINES, 48, 128), F32),
        in_specs=[lines(N, 128, count=PAIR), *projected(PAIR), whole((128 * 24, N)), MATRIX],
        out_specs=pl.BlockSpec((16, PAIR, 48, 128), lambda i: (0, i, 0, 0)),
        scratch_shapes=[pltpu.VMEM((HEADS, N, N), F32), pltpu.VMEM((PAIR, 128, N), F32)],
        compiler_params=PARAMS,
        name="end_attention",
    )(end_lines, *end_parts, end_bias, end_out)
    returned = lax.all_to_all(second, ROW, split_axis=0, concat_axis=0, tiled=True)
    return jnp.transpose(returned, (2, 0, 1, 3)).reshape(48, 96, 128)


def solution(mesh):
    parts = Mesh(mesh.devices.reshape(4, 2, 2, 4, 2), ("z", "x_hi", "core", "y", "x_lo"))
    return jax.shard_map(
        local,
        mesh=parts,
        in_specs=(P(ROW, COL, None), P(ROW, COL), P(), P(), P(), P(), P(), P()),
        out_specs=P(ROW, COL, None),
        check_vma=False,
    )
```

time: 311 us -> 298 us (0.958)
  blocking collectives: 58.1 us -> 35.7 us
  waiting for transfers between devices: 94.8 us -> 104 us
  starting transfers between devices: 7.83 us -> 16.8 us
  local copies, waits for them, and re-layouts: 20.5 us -> 11.8 us
    all_to_all x2 -> x0, blocking collectives: 22.5 us -> none  [the longest x1 11.6 us: local(): lax.all_to_all(ends_mask, ROW, split_axis=0, concat_axis=0, tiled=True)]
    all_to_all x1, waiting for transfers between devices: 18.2 us -> 25.3 us  [local(): rows = lax.all_to_all(parts, COL, split_axis=0, concat_axis=0, tiled=True)]
    reshape x4 -> x3, local copies, waits for them, and re-layouts: 6.43 us -> 0.52 us  [the longest x2 0.3 us: local(): jnp.transpose(sent_mask, (2, 0, 1, 3)).reshape(128, LINES * LINES)]
    ppermute x0 -> x3, starting transfers between devices: none -> 5.21 us  [gather_start(): lax.ppermute(shard, 'y', [(t, (t + hop) % 4) for t in range(4)])]
    all_gather x2, waiting for transfers between devices: 47.4 us -> 43.1 us  [the longest x1 31.2 us: gather_end(): lax.all_gather(shard, ('z', 'x_hi', 'x_lo', 'y', 'core'), axis=0, tiled=T...]
    all_to_all x1, starting transfers between devices: 3.86 us -> 7.47 us  [local(): lax.all_to_all(first_pair.reshape(128, SLOT, 128), EVERY, split_axis=0, c...]
    ppermute x0 -> x3, waiting for transfers between devices: none -> 3.41 us  [gather_start(): lax.ppermute(shard, 'y', [(t, (t + hop) % 4) for t in range(4)])]
    all_to_all x1, waiting for transfers between devices: 29.2 us -> 32.6 us  [local(): lax.all_to_all(first_pair.reshape(128, SLOT, 128), EVERY, split_axis=0, c...]
  transfers between devices with their start and end apart: 4 -> 7, of which waited for: 4 -> 6; matrix products, arithmetic and copies ran while one was open for 6% -> 4% of each run, Pallas kernels for 7% -> 7%
where the time goes in v3:
time: 298 us; the launch traced here: 297 us
  Pallas kernels  107 us (36%)
  waiting for transfers between devices  104 us (35%)
  blocking collectives  35.7 us (12%)
  starting transfers between devices  16.8 us (6%)
  between operations  13.6 us (5%)
  local copies, waits for them, and re-layouts  11.8 us (4%)
  other arithmetic  7.88 us (3%)
    pallas_call x1, Pallas kernels, local(): pl.pallas_call(start_kernel, grid=(LINES // PAIR,), out_shape=(jax.ShapeD...  47.4 us
    all_to_all x1, blocking collectives, local(): lax.all_to_all(second, ROW, split_axis=0, concat_axis=0, tiled=True)  35.7 us
    pallas_call x1, Pallas kernels, local(): pl.pallas_call(end_kernel, grid=(LINES // PAIR,), out_shape=jax.ShapeDtyp...  32.9 us
    all_to_all x1, waiting for transfers between devices, local(): lax.all_to_all(first_pair.reshape(128, SLOT, 128), EVERY, split_axis=0, c...  32.6 us
    all_gather x1, waiting for transfers between devices, gather_end(): lax.all_gather(shard, ('z', 'x_hi', 'x_lo', 'y', 'core'), axis=0, tiled=T...  31.2 us
    all_to_all x1, waiting for transfers between devices, local(): rows = lax.all_to_all(parts, COL, split_axis=0, concat_axis=0, tiled=True)  25.3 us
    all_gather x1, waiting for transfers between devices, gather_start(): lax.all_gather(blocks, ('z', 'x_hi', 'x_lo', 'core'), axis=0, tiled=True)  11.9 us
    pallas_call x1, Pallas kernels, local(): pl.pallas_call(end_project_kernel, grid=(LINES,), out_shape=PROJECTED_SHA...  10.5 us
  transfers between devices with their start and end apart: 7, of which 6 were waited for; matrix products, arithmetic and copies ran while one was open for 4% of the time, Pallas kernels for 7%

profile of v3, /device:TPU:1, one launch (start us, length us, event | category | flops | bytes accessed | tf_op | source)
XLA Modules:
  0.0 297.2 jit_solution(11029007705184415504)
XLA Ops:
  6.5 1.5 copy.16.w_bias
  8.0 6.1 %tile_bias.1 = (f32[144,128]{1,0:T(8,128)}, f32[8,584,128]{2,1,0:T(8,128)}) custom-call(s32[768]{0:T(1024)} %ids.1, f32[2,4]{1,0:T(2,128)} %chain_gain.1, f32[48,96,128]{2,1,0:T(8,128)} %pair_ref.1, s32[48,96]{1,0:T(8,128)} %mask_ref.1, f32[2,128]{1,0:T(2,128)} %gain.1, f32[2,128,4]{2,1,0:T(8,128)} %copy.16.w_bias), custom_call_target="tpu_custom_call" | custom-call | tf_op jit(solution)/shard_map/tile_bias/pallas_call | solution.py:297
  14.1 2.1 collective-permute-start
  16.2 1.4 collective-permute-start.1
  17.7 1.6 collective-permute-start.2
  19.6 3.1 %collective-permute-done.2 = f32[144,128]{1,0:T(8,128)S(1)} collective-permute-done((f32[144,128]{1,0:T(8,128)}, f32[144,128]{1,0:T(8,128)S(1)}, u32[]{:S(2)}, u32[]{:S(2)}) %collective-permute-start.2) | collective-permute-done | bytes 73760 | tf_op jit(solution)/shard_map/ppermute | solution.py:48
  22.7 1.6 pad_maximum_fusion
  24.4 3.9 %all-to-all-start = ((f32[8,584,128]{2,1,0:T(8,128)}), f32[8,584,128]{2,1,0:T(8,128)S(1)}, u32[]{:S(2)}, u32[]{:S(2)}) async-start(f32[8,584,128]{2,1,0:T(8,128)} %get-tuple-element.18), calls=%async_computation | async-start | bytes 4784128 | tf_op jit(solution)/shard_map/all_to_all | solution.py:314
  28.6 1.1 fusion.4
  29.9 0.8 copy.21.w_key
  31.5 0.7 maximum_bitcast_fusion.w_query
  32.1 0.7 maximum_bitcast_fusion.1.w_value
  33.4 0.7 pad_maximum_fusion.2.w_out
  34.7 0.7 compare_convert_fusion.same
  35.4 25.3 %all-to-all-done.x_ref.mask_ref = f32[8,584,128]{2,1,0:T(8,128)S(1)} async-done(((f32[8,584,128]{2,1,0:T(8,128)}), f32[8,584,128]{2,1,0:T(8,128)S(1)}, u32[]{:S(2)}, u32[]{:S(2)}) %all-to-all-start) | async-done | bytes 2392096 | tf_op jit(solution)/shard_map/all_to_all | solution.py:314
  60.9 0.7 copy.18
  62.5 10.2 %start_projections.1 = (bf16[6,4,128,768]{3,2,1,0:T(8,128)(2,1)}, bf16[6,4,768,128]{3,2,1,0:T(8,128)(2,1)}, bf16[6,4,80,768]{3,2,1,0:T(8,128)(2,1)}, f32[6,128,768]{2,1,0:T(8,128)}) custom-call(f32[8,584,128]{2,1,0:T(8,128)} %copy-done, f32[8,584,128]{2,1,0:T(8,128)} %copy-done, bf16[256,256]{1,0:T(8,128)(2,1)} %maximum_bitcast_fusion.w_query, ...), custom_call_target="tpu_custom_call" | custom-call | tf_op jit(solution)/shard_map/start_projections/pallas_call | solution.py:322
  72.7 11.9 %all-gather.3.cloned.1.call-done.gathered = f32[18432,128]{1,0:T(8,128)} async-done(((f32[576,128]{1,0:T(8,128)}), f32[18432,128]{1,0:T(8,128)}) %all-gather.3.cloned.1.call-update) | async-done | bytes 9437200 | tf_op jit(solution)/shard_map/all_gather | solution.py:50
  85.3 47.4 %start_attention.1 = (f32[5120,128]{1,0:T(8,128)}, f32[24,768]{1,0:T(8,128)}) custom-call(f32[8,584,128]{2,1,0:T(8,128)} %copy-done, f32[128,128]{1,0:T(8,128)} %pad.6.mask_ref, bf16[6,4,128,768]{3,2,1,0:T(8,128)(2,1)} %get-tuple-element.19.query, bf16[6,4,768,128]{3,2,1,0:T(8,128)(2,1)} %get-tuple-element.20.key, ...), custom_call_target="tpu_custom_call" | custom-call | tf_op jit(solution)/shard_map/start_attention/pallas_call | solution.py:336
  132.8 7.5 %all-to-all-start.1 = ((f32[128,40,128]{2,1,0:T(8,128)}), f32[128,40,128]{2,1,0:T(8,128)S(1)}, u32[]{:S(2)}, u32[]{:S(2)}) async-start(f32[128,40,128]{2,1,0:T(8,128)} %bitcast.44), calls=%async_computation.1 | async-start | bytes 5242880 | tf_op jit(solution)/shard_map/all_to_all | solution.py:359
  140.4 0.8 copy.23.w_key
  141.2 0.7 maximum_bitcast_fusion.3.w_query
  141.9 0.7 maximum_bitcast_fusion.4.w_value
  142.6 0.7 maximum_bitcast_fusion.5.w_gate
  143.3 0.7 pad_maximum_fusion.4.w_out
  143.9 32.6 %all-to-all-done.1 = f32[128,40,128]{2,1,0:T(8,128)S(1)} async-done(((f32[128,40,128]{2,1,0:T(8,128)}), f32[128,40,128]{2,1,0:T(8,128)S(1)}, u32[]{:S(2)}, u32[]{:S(2)}) %all-to-all-start.1) | async-done | bytes 2621472 | tf_op jit(solution)/shard_map/all_to_all | solution.py:359
  176.5 1.5 copy-done.1
  178.0 10.5 %end_projections.1 = (bf16[6,4,128,768]{3,2,1,0:T(8,128)(2,1)}, bf16[6,4,768,128]{3,2,1,0:T(8,128)(2,1)}, bf16[6,4,80,768]{3,2,1,0:T(8,128)(2,1)}, f32[6,128,768]{2,1,0:T(8,128)}, f32[6,768,128]{2,1,0:T(8,128)}) custom-call(f32[5120,128]{1,0:T(8,128)} %bitcast.42, bf16[256,256]{1,0:T(8,128)(2,1)} %maximum_bitcast_fusion.3.w_query, ...), custom_call_target="tpu_custom_call" | custom-call | tf_op jit(solution)/shard_map/end_projections/pallas_call | solution.py:362
  188.5 31.2 %all-gather.5.cloned.1.call-done.gathered = f32[3072,768]{1,0:T(8,128)} async-done(((f32[24,768]{1,0:T(8,128)}), f32[3072,768]{1,0:T(8,128)}) %all-gather.5.cloned.1.call-update) | async-done | bytes 9437200 | tf_op jit(solution)/shard_map/all_gather | solution.py:58
  219.7 32.9 %end_attention.1 = f32[16,6,48,128]{3,2,1,0:T(8,128)} custom-call(f32[6,768,128]{2,1,0:T(8,128)} %get-tuple-element.25.x_ref, bf16[6,4,128,768]{3,2,1,0:T(8,128)(2,1)} %get-tuple-element.26.query, bf16[6,4,768,128]{3,2,1,0:T(8,128)(2,1)} %get-tuple-element.27.key, bf16[6,4,80,768]{3,2,1,0:T(8,128)(2,1)} %get-tuple-element.28.value, ...), custom_call_target="tpu_custom_call" | custom-call | tf_op jit(solution)/shard_map/end_attention/pallas_call | solution.py:372
  252.6 35.7 %all_to_all.15 = f32[16,6,48,128]{3,2,1,0:T(8,128)S(1)} all-to-all(f32[16,6,48,128]{3,2,1,0:T(8,128)} %end_attention.1), channel_id=1, replica_groups=mesh['z'=4,'x_hi'=2,'core'=2,'y'=4,'x_lo'=2] {'z','x_hi','core'}, dimensions={0} | all-to-all | bytes 4718592 | tf_op jit(solution)/shard_map/all_to_all | solution.py:382
  288.3 2.1 copy.24
  (48 shorter events, 4.8 us)
Async XLA Ops:
  6.5 78.1 %all-gather.3.cloned.1.call-start = ((), (), s32[]{:S(2)}) async-start(), calls=%async_computation.3 | async-start | bytes 9732096 | tf_op jit(solution)/shard_map/all_gather | solution.py:50
  14.1 5.5 %collective-permute-start = (f32[144,128]{1,0:T(8,128)}, f32[144,128]{1,0:T(8,128)S(1)}, u32[]{:S(2)}, u32[]{:S(2)}) collective-permute-start(f32[144,128]{1,0:T(8,128)} %get-tuple-element.23), channel_id=1, source_target_pairs={{0,2},{2,4},{4,6},{6,0},{1,3},{3,5},{5,7},{7,1},{8,10},{10,12},{12... | collective-permute-start | bytes 221192 | tf_op jit(solution)/shard_map/ppermute | solution.py:48
  16.2 3.4 %collective-permute-start.1 = (f32[144,128]{1,0:T(8,128)}, f32[144,128]{1,0:T(8,128)S(1)}, u32[]{:S(2)}, u32[]{:S(2)}) collective-permute-start(f32[144,128]{1,0:T(8,128)} %get-tuple-element.23), channel_id=1, source_target_pairs={{0,6},{2,0},{4,2},{6,4},{1,7},{3,1},{5,3},{7,5},{8,14},{10,8},{12,... | collective-permute-start | bytes 221192 | tf_op jit(solution)/shard_map/ppermute | solution.py:48
  17.7 5.1 %collective-permute-start.2 = (f32[144,128]{1,0:T(8,128)}, f32[144,128]{1,0:T(8,128)S(1)}, u32[]{:S(2)}, u32[]{:S(2)}) collective-permute-start(f32[144,128]{1,0:T(8,128)} %get-tuple-element.23), channel_id=1, source_target_pairs={{0,4},{2,6},{4,0},{6,2},{1,5},{3,7},{5,1},{7,3},{8,12},{10,14},{12... | collective-permute-start | bytes 221192 | tf_op jit(solution)/shard_map/ppermute | solution.py:48
  24.4 6.3 %copy-start.3 = (s32[768]{0:T(1024)S(1)}, s32[768]{0:T(1024)}, u32[]{:S(2)}) copy-start(s32[768]{0:T(1024)} %ids.1) | copy-start | bytes 9220
  24.4 6.3 %copy-start.4 = (f32[2,128,4]{1,2,0:T(4,128)S(1)}, f32[2,128,4]{1,2,0:T(4,128)}, u32[]{:S(2)}) copy-start(f32[2,128,4]{1,2,0:T(4,128)} %param.13) | copy-start | bytes 12292
  24.4 6.9 %copy-start.6 = (f32[2,4]{1,0:T(2,128)S(1)}, f32[2,4]{1,0:T(2,128)}, u32[]{:S(2)}) copy-start(f32[2,4]{1,0:T(2,128)} %chain_gain.1) | copy-start | bytes 100
  24.4 36.2 %all-to-all-start = ((f32[8,584,128]{2,1,0:T(8,128)}), f32[8,584,128]{2,1,0:T(8,128)S(1)}, u32[]{:S(2)}, u32[]{:S(2)}) async-start(f32[8,584,128]{2,1,0:T(8,128)} %get-tuple-element.18), calls=%async_computation | async-start | bytes 4784128 | tf_op jit(solution)/shard_map/all_to_all | solution.py:314
  28.3 3.0 %copy-start.2 = (f32[2,128,128]{2,1,0:T(8,128)S(1)}, f32[2,128,128]{2,1,0:T(8,128)}, u32[]{:S(2)}) copy-start(f32[2,128,128]{2,1,0:T(8,128)} %param.14) | copy-start | bytes 393220
  28.4 5.8 %copy-start.5 = (f32[2,128]{1,0:T(2,128)S(1)}, f32[2,128]{1,0:T(2,128)}, u32[]{:S(2)}) copy-start(f32[2,128]{1,0:T(2,128)} %gain.1) | copy-start | bytes 3076
  28.4 191.3 %all-gather.5.cloned.1.call-start = ((), (), s32[]{:S(2)}) async-start(), calls=%async_computation.4 | async-start | bytes 9510912 | tf_op jit(solution)/shard_map/all_gather | solution.py:58
  60.6 1.9 copy-start
  132.8 43.7 %all-to-all-start.1 = ((f32[128,40,128]{2,1,0:T(8,128)}), f32[128,40,128]{2,1,0:T(8,128)S(1)}, u32[]{:S(2)}, u32[]{:S(2)}) async-start(f32[128,40,128]{2,1,0:T(8,128)} %bitcast.44), calls=%async_computation.1 | async-start | bytes 5242880 | tf_op jit(solution)/shard_map/all_to_all | solution.py:359
  176.5 1.5 copy-start.1
Sparse Core Ops, SparseCore 0:
  24.5 60.1 all-gather.2
  132.9 86.7 all-gather.4

commit v4 on v3

--- a/solution.py
+++ b/solution.py
@@ -58,45 +58,54 @@
     return lax.all_gather(shard, ("z", "x_hi", "x_lo", "y", "core"), axis=0, tiled=True)
 
 
-def order_tiles(gathered, bias):
+def fetch(gathered, held, sems):
+    size = held.shape[0] // 8
+    copies = []
+    for t in range(8):
+        inside = pl.ds(t * size, size)
+        copies.append(pltpu.make_async_copy(gathered.at[inside], held.at[inside], sems.at[t]))
+        copies[-1].start()
+    return copies
+
+
+def order_tiles(copies, held, bias):
     slot = lax.broadcasted_iota(jnp.int32, (1, 128), 1) // 16
-
-    def step(col, _):
-        for tile in range(6):
+    arrived = 0
+    for tile in range(6):
+        while arrived <= (tile * 8 + 7) // 3 // 2:
+            copies[arrived].wait()
+            arrived += 1
+
+        def step(col, _):
             pieces = []
             for t in range(8):
                 row, part = divmod(tile * 8 + t, 3)
                 start = pl.multiple_of(start_place(row, col) * 144 + part * 48, 8)
-                pieces.append(gathered[pl.ds(start, 48), :])
-            for distance in (4, 2, 1):
-                upper = (slot // distance) % 2 == 1
-                moved = list(pieces)
-                for t in range(8):
-                    if (t // distance) % 2 == 0:
-                        one, two = pieces[t], pieces[t + distance]
-                        moved[t] = jnp.where(upper, pltpu.roll(two, 16 * distance, 1), one)
-                        moved[t + distance] = jnp.where(upper, two, pltpu.roll(one, 128 - 16 * distance, 1))
-                pieces = moved
+                pieces.append(held[pl.ds(start, 48), :])
+            for hop in (1, 2, 4):
+                upper = (slot // hop) % 2 == 1
+                pieces = [jnp.where(upper, pieces[(t + hop) % 8], pieces[t]) for t in range(8)]
             for t in range(8):
                 start = pl.multiple_of(col * 96 + (t // 4) * 48, 8)
-                bias[t % 4, pl.ds(start, 48), tile * 128 : (tile + 1) * 128] = pieces[t]
-        return 0
-
-    lax.fori_loop(0, 8, step, 0)
-
-
-def order_lines(gathered, bias):
-    def step(outer, _):
+                turned = pieces[(8 - t) % 8]
+                if t:
+                    turned = pltpu.roll(turned, 128 - 16 * t, 1)
+                bias[t % 4, pl.ds(start, 48), tile * 128 : (tile + 1) * 128] = turned
+            return 0
+
+        lax.fori_loop(0, 8, step, 0)
+
+
+def order_lines(copies, held, bias):
+    for outer in range(8):
+        copies[outer].wait()
         for part in range(4):
             owners = [end_place(outer * 2 + part // 2, (part % 2) * 4 + t) for t in range(4)]
-            blocks = [gathered[pl.ds(pl.multiple_of(owner * 24, 8), 24), :] for owner in owners]
-            start = pl.multiple_of(outer * 96 + part * 24, 8)
+            blocks = [held[owner * 24 : owner * 24 + 24, :] for owner in owners]
+            start = outer * 96 + part * 24
             for head in range(HEADS):
                 rows = [block[head * LINES : (head + 1) * LINES] for block in blocks]
-                bias[head, pl.ds(start, 24), :] = jnp.concatenate(rows, axis=0)
-        return 0
-
-    lax.fori_loop(0, 8, step, 0)
+                bias[head, start : start + 24, :] = jnp.concatenate(rows, axis=0)
 
 
 def tile_kernel(ids, chain_gain, pair_ref, mask_ref, gain, w_bias, out_ref, parts_ref, normed):
@@ -108,7 +117,8 @@
     normed[...] = layer_norm(pair_ref[...].reshape(48 * 96, 128), gain[:1])
     lane = lax.broadcasted_iota(jnp.int32, (128, 128), 1)
     head = (lane // 16) % 4
-    w_lanes = sum(jnp.where(head == t, w_bias[0][:, t : t + 1] * LOG2E, 0.0) for t in range(HEADS))
+    columns = jnp.concatenate([w_bias[0], w_bias[0]], axis=0).T
+    w_lanes = sum(jnp.where(head == t, columns[:, t : t + 1] * LOG2E, 0.0) for t in range(HEADS))
     first_row, first_col = lax.axis_index(ROW) * 48, lax.axis_index(COL) * 96
     wide = lane[:1]
     gains = sum(jnp.where(head[:1] == t, chain_gain[0, t] * LOG2E, 0.0) for t in range(HEADS))
@@ -134,7 +144,9 @@
         total = total + jnp.dot(
             jnp.concatenate(rows, axis=0), weights, precision=lax.Precision.HIGHEST, preferred_element_type=F32
         )
-    out_ref[...] = total
+    for part in range(3):
+        before = lax.rem(lax.axis_index(ROW) * 3 + part, 8)
+        out_ref[part * 48 : part * 48 + 48] = pltpu.roll(total[part * 48 : part * 48 + 48], before * 16, 1)
 
 
 def project(x, mask, w_query, w_key, w_value, w_gate, gain, query, key, value, gate):
@@ -216,17 +228,21 @@
 
 
 def start_kernel(
-    x_ref, mask_ref, query, key, value, gate, gathered, w_out, end_gain, w_bias, chain, same, pair_ref, bias_ref, bias, mixed, line
+    x_ref, mask_ref, query, key, value, gate, gathered, w_out, end_gain, w_bias, chain_gain, same,
+    pair_ref, bias_ref, bias, mixed, line, held, sems,
 ):
     step = pl.program_id(0)
 
     @pl.when(step == 0)
     def _():
-        order_tiles(gathered, bias)
+        copies = fetch(gathered, held, sems)
         pair_ref[...] = jnp.zeros_like(pair_ref)
         for group in range(16):
             pair_ref[pl.ds(group * 8 * SLOT + LINES * LINES, 8, stride=SLOT), :] = mask_ref[group * 8 : group * 8 + 8]
-
+        order_tiles(copies, held, bias)
+
+    place = lax.broadcasted_iota(jnp.int32, (8, 1), 0)
+    chain = sum(jnp.where(place == t, chain_gain[1, t], 0.0) for t in range(HEADS))
     for t in range(PAIR):
         first = x_ref[...].reshape(N, 128) + attend(t, query, key, value, gate, bias, w_out, mixed)
         line[t] = first
@@ -240,15 +256,15 @@
         plane = lax.dot_general(
             w_bias[...], normed, NT, precision=lax.Precision.HIGHEST, preferred_element_type=F32
         )
-        plane = (plane + chain[:, :1] * same[t]) * LOG2E
+        plane = (plane + chain * same[t]) * LOG2E
         for head in range(HEADS):
             bias_ref[pl.ds(head * LINES + here, 1), :] = plane[head : head + 1]
 
 
-def end_kernel(x_ref, query, key, value, gate, gathered, w_out, out_ref, bias, mixed):
+def end_kernel(x_ref, query, key, value, gate, gathered, w_out, out_ref, bias, mixed, held, sems):
     @pl.when(pl.program_id(0) == 0)
     def _():
-        order_lines(gathered, bias)
+        order_lines(fetch(gathered, held, sems), held, bias)
 
     for t in range(PAIR):
         update = attend(t, query, key, value, gate, bias, w_out, mixed)
@@ -308,7 +324,7 @@
         scratch_shapes=[pltpu.VMEM((48 * 96, 128), F32)],
         compiler_params=PARAMS,
         name="tile_bias",
-    )(chain_ids, chain_gain, pair_state, pair_mask, ln_gain, w_bias)
+    )(chain_ids, chain_gain, pair_state, pair_mask, ln_gain, jnp.swapaxes(w_bias, 1, 2))
     start_bias = gather_start(tile_bias)
 
     rows = lax.all_to_all(parts, COL, split_axis=0, concat_axis=0, tiled=True)
@@ -332,7 +348,6 @@
     ids_line = lax.dynamic_slice(chain_ids, (row * 48 + col * LINES,), (LINES,))
     same_line = (ids_line[:, None] == chain_ids[None, :]).astype(F32).reshape(LINES, 1, N)
     end_w = jnp.concatenate([w_bias[1].T, jnp.zeros((4, 128), F32)], axis=0)
-    chain = jnp.broadcast_to(jnp.concatenate([chain_gain[1], jnp.zeros((4,), F32)])[:, None], (8, 128))
     first_pair, end_shard = pl.pallas_call(
         start_kernel,
         grid=(LINES // PAIR,),
@@ -342,18 +357,20 @@
         ),
         in_specs=[
             row_block, whole((128, 128)),
-            *projected(PAIR), whole((128 * 144, 128)), MATRIX,
-            whole((1, 128)), whole((8, 128)), whole((8, 128)), lines(1, N, count=PAIR),
+            *projected(PAIR), pl.BlockSpec(memory_space=pl.ANY), MATRIX,
+            whole((1, 128)), whole((8, 128)), pl.BlockSpec(memory_space=pltpu.SMEM), lines(1, N, count=PAIR),
         ],
         out_specs=(whole((128 * SLOT, 128)), whole((HEADS * LINES, N))),
         scratch_shapes=[
             pltpu.VMEM((HEADS, N, N), F32),
             pltpu.VMEM((PAIR, 128, N), F32),
             pltpu.VMEM((PAIR, N, 128), F32),
+            pltpu.VMEM((128 * 144, 128), F32),
+            pltpu.SemaphoreType.DMA((8,)),
         ],
         compiler_params=PARAMS,
         name="start_attention",
-    )(rows, sent_mask, *start_parts, start_bias, start_out, ln_gain[1:2], end_w, chain, same_line)
+    )(rows, sent_mask, *start_parts, start_bias, start_out, ln_gain[1:2], end_w, chain_gain, same_line)
 
     end_bias = gather_end(end_shard)
     columns = lax.all_to_all(
@@ -373,9 +390,14 @@
         end_kernel,
         grid=(LINES // PAIR,),
         out_shape=jax.ShapeDtypeStruct((16, LINES, 48, 128), F32),
-        in_specs=[lines(N, 128, count=PAIR), *projected(PAIR), whole((128 * 24, N)), MATRIX],
+        in_specs=[lines(N, 128, count=PAIR), *projected(PAIR), pl.BlockSpec(memory_space=pl.ANY), MATRIX],
         out_specs=pl.BlockSpec((16, PAIR, 48, 128), lambda i: (0, i, 0, 0)),
-        scratch_shapes=[pltpu.VMEM((HEADS, N, N), F32), pltpu.VMEM((PAIR, 128, N), F32)],
+        scratch_shapes=[
+            pltpu.VMEM((HEADS, N, N), F32),
+            pltpu.VMEM((PAIR, 128, N), F32),
+            pltpu.VMEM((128 * 24, N), F32),
+            pltpu.SemaphoreType.DMA((8,)),
+        ],
         compiler_params=PARAMS,
         name="end_attention",
     )(end_lines, *end_parts, end_bias, end_out)

time: 298 us -> 289 us (0.970)
  Pallas kernels: 107 us -> 101 us
    pallas_call x1, Pallas kernels: 47.4 us -> 41.2 us  [local(): pl.pallas_call(start_kernel, grid=(LINES // PAIR,), out_shape=(jax.ShapeD...]
where the time goes in v4:
time: 289 us; the launch traced here: 288 us
  waiting for transfers between devices  105 us (36%)
  Pallas kernels  101 us (35%)
  blocking collectives  35.7 us (12%)
  starting transfers between devices  16.6 us (6%)
  between operations  13.6 us (5%)
  local copies, waits for them, and re-layouts  9.53 us (3%)
  other arithmetic  7.84 us (3%)
    pallas_call x1, Pallas kernels, local(): pl.pallas_call(start_kernel, grid=(LINES // PAIR,), out_shape=(jax.ShapeD...  41.2 us
    all_to_all x1, blocking collectives, local(): lax.all_to_all(second, ROW, split_axis=0, concat_axis=0, tiled=True)  35.7 us
    all_to_all x1, waiting for transfers between devices, local(): lax.all_to_all(first_pair.reshape(128, SLOT, 128), EVERY, split_axis=0, c...  32.6 us
    pallas_call x1, Pallas kernels, local(): pl.pallas_call(end_kernel, grid=(LINES // PAIR,), out_shape=jax.ShapeDtyp...  32.5 us
    all_gather x1, waiting for transfers between devices, gather_end(): lax.all_gather(shard, ('z', 'x_hi', 'x_lo', 'y', 'core'), axis=0, tiled=T...  31.2 us
    all_to_all x1, waiting for transfers between devices, local(): rows = lax.all_to_all(parts, COL, split_axis=0, concat_axis=0, tiled=True)  25.3 us
    all_gather x1, waiting for transfers between devices, gather_start(): lax.all_gather(blocks, ('z', 'x_hi', 'x_lo', 'core'), axis=0, tiled=True)  12.1 us
    pallas_call x1, Pallas kernels, local(): pl.pallas_call(end_project_kernel, grid=(LINES,), out_shape=PROJECTED_SHA...  10.5 us
  transfers between devices with their start and end apart: 7, of which 6 were waited for; matrix products, arithmetic and copies ran while one was open for 4% of the time, Pallas kernels for 7%

profile of v4, /device:TPU:1, one launch (start us, length us, event | category | flops | bytes accessed | tf_op | source)
XLA Modules:
  0.0 288.5 jit_solution(9422241225178542097)
XLA Ops:
  6.5 6.1 %tile_bias.1 = (f32[144,128]{1,0:T(8,128)}, f32[8,584,128]{2,1,0:T(8,128)}) custom-call(s32[768]{0:T(1024)} %ids.1, f32[2,4]{1,0:T(2,128)} %chain_gain.3, f32[48,96,128]{2,1,0:T(8,128)} %pair_ref.1, s32[48,96]{1,0:T(8,128)} %mask_ref.1, f32[2,128]{1,0:T(2,128)} %gain.1, f32[2,4,128]{2,1,0:T(4,128)} %bitcast.47), custom_call_target="tpu_custom_call" | custom-call | tf_op jit(solution)/shard_map/tile_bias/pallas_call | solution.py:313
  12.6 2.1 collective-permute-start
  14.8 1.4 collective-permute-start.1
  16.2 1.6 collective-permute-start.2
  18.2 3.1 %collective-permute-done.2 = f32[144,128]{1,0:T(8,128)S(1)} collective-permute-done((f32[144,128]{1,0:T(8,128)}, f32[144,128]{1,0:T(8,128)S(1)}, u32[]{:S(2)}, u32[]{:S(2)}) %collective-permute-start.2) | collective-permute-done | bytes 73760 | tf_op jit(solution)/shard_map/ppermute | solution.py:48
  21.3 1.6 pad_maximum_fusion
  23.0 3.8 %all-to-all-start = ((f32[8,584,128]{2,1,0:T(8,128)}), f32[8,584,128]{2,1,0:T(8,128)S(1)}, u32[]{:S(2)}, u32[]{:S(2)}) async-start(f32[8,584,128]{2,1,0:T(8,128)} %get-tuple-element.18), calls=%async_computation | async-start | bytes 4784128 | tf_op jit(solution)/shard_map/all_to_all | solution.py:330
  27.0 1.1 fusion.4
  28.3 0.8 copy.19.w_key
  29.8 0.7 maximum_bitcast_fusion.w_query
  30.5 0.7 maximum_bitcast_fusion.1.w_value
  31.1 0.7 maximum_bitcast_fusion.2.w_gate
  31.8 0.7 pad_maximum_fusion.2.w_out
  33.0 0.7 compare_convert_fusion.same
  33.7 25.3 %all-to-all-done.x_ref.mask_ref = f32[8,584,128]{2,1,0:T(8,128)S(1)} async-done(((f32[8,584,128]{2,1,0:T(8,128)}), f32[8,584,128]{2,1,0:T(8,128)S(1)}, u32[]{:S(2)}, u32[]{:S(2)}) %all-to-all-start) | async-done | bytes 2392096 | tf_op jit(solution)/shard_map/all_to_all | solution.py:330
  59.2 0.7 copy.16
  60.9 10.2 %start_projections.1 = (bf16[6,4,128,768]{3,2,1,0:T(8,128)(2,1)}, bf16[6,4,768,128]{3,2,1,0:T(8,128)(2,1)}, bf16[6,4,80,768]{3,2,1,0:T(8,128)(2,1)}, f32[6,128,768]{2,1,0:T(8,128)}) custom-call(f32[8,584,128]{2,1,0:T(8,128)} %copy-done, f32[8,584,128]{2,1,0:T(8,128)} %copy-done, bf16[256,256]{1,0:T(8,128)(2,1)} %maximum_bitcast_fusion.w_query, ...), custom_call_target="tpu_custom_call" | custom-call | tf_op jit(solution)/shard_map/start_projections/pallas_call | solution.py:338
  71.1 12.1 %all-gather.3.cloned.1.call-done.gathered = f32[18432,128]{1,0:T(8,128)} async-done(((f32[576,128]{1,0:T(8,128)}), f32[18432,128]{1,0:T(8,128)}) %all-gather.3.cloned.1.call-update) | async-done | bytes 9437200 | tf_op jit(solution)/shard_map/all_gather | solution.py:50
  83.2 41.2 %start_attention.1 = (f32[5120,128]{1,0:T(8,128)}, f32[24,768]{1,0:T(8,128)}) custom-call(f32[8,584,128]{2,1,0:T(8,128)} %copy-done, f32[128,128]{1,0:T(8,128)} %pad.5.mask_ref, bf16[6,4,128,768]{3,2,1,0:T(8,128)(2,1)} %get-tuple-element.19.query, bf16[6,4,768,128]{3,2,1,0:T(8,128)(2,1)} %get-tuple-element.20.key, ...), custom_call_target="tpu_custom_call" | custom-call | tf_op jit(solution)/shard_map/start_attention/pallas_call | solution.py:351
  124.5 7.4 %all-to-all-start.1 = ((f32[128,40,128]{2,1,0:T(8,128)}), f32[128,40,128]{2,1,0:T(8,128)S(1)}, u32[]{:S(2)}, u32[]{:S(2)}) async-start(f32[128,40,128]{2,1,0:T(8,128)} %bitcast.43), calls=%async_computation.1 | async-start | bytes 5242880 | tf_op jit(solution)/shard_map/all_to_all | solution.py:376
  132.1 0.8 copy.21.w_key
  132.9 0.7 maximum_bitcast_fusion.3.w_query
  133.5 0.7 maximum_bitcast_fusion.4.w_value
  134.2 0.7 maximum_bitcast_fusion.5.w_gate
  134.9 0.7 pad_maximum_fusion.4.w_out
  135.5 32.6 %all-to-all-done.1 = f32[128,40,128]{2,1,0:T(8,128)S(1)} async-done(((f32[128,40,128]{2,1,0:T(8,128)}), f32[128,40,128]{2,1,0:T(8,128)S(1)}, u32[]{:S(2)}, u32[]{:S(2)}) %all-to-all-start.1) | async-done | bytes 2621472 | tf_op jit(solution)/shard_map/all_to_all | solution.py:376
  168.1 1.5 copy-done.1
  169.6 10.5 %end_projections.1 = (bf16[6,4,128,768]{3,2,1,0:T(8,128)(2,1)}, bf16[6,4,768,128]{3,2,1,0:T(8,128)(2,1)}, bf16[6,4,80,768]{3,2,1,0:T(8,128)(2,1)}, f32[6,128,768]{2,1,0:T(8,128)}, f32[6,768,128]{2,1,0:T(8,128)}) custom-call(f32[5120,128]{1,0:T(8,128)} %bitcast.41, bf16[256,256]{1,0:T(8,128)(2,1)} %maximum_bitcast_fusion.3.w_query, ...), custom_call_target="tpu_custom_call" | custom-call | tf_op jit(solution)/shard_map/end_projections/pallas_call | solution.py:379
  180.1 31.2 %all-gather.5.cloned.1.call-done.gathered = f32[3072,768]{1,0:T(8,128)} async-done(((f32[24,768]{1,0:T(8,128)}), f32[3072,768]{1,0:T(8,128)}) %all-gather.5.cloned.1.call-update) | async-done | bytes 9437200 | tf_op jit(solution)/shard_map/all_gather | solution.py:58
  211.3 32.5 %end_attention.1 = f32[16,6,48,128]{3,2,1,0:T(8,128)} custom-call(f32[6,768,128]{2,1,0:T(8,128)} %get-tuple-element.25.x_ref, bf16[6,4,128,768]{3,2,1,0:T(8,128)(2,1)} %get-tuple-element.26.query, bf16[6,4,768,128]{3,2,1,0:T(8,128)(2,1)} %get-tuple-element.27.key, bf16[6,4,80,768]{3,2,1,0:T(8,128)(2,1)} %get-tuple-element.28.value, ...), custom_call_target="tpu_custom_call" | custom-call | tf_op jit(solution)/shard_map/end_attention/pallas_call | solution.py:389
  243.8 35.7 %all_to_all.15 = f32[16,6,48,128]{3,2,1,0:T(8,128)S(1)} all-to-all(f32[16,6,48,128]{3,2,1,0:T(8,128)} %end_attention.1), channel_id=1, replica_groups=mesh['z'=4,'x_hi'=2,'core'=2,'y'=4,'x_lo'=2] {'z','x_hi','core'}, dimensions={0} | all-to-all | bytes 4718592 | tf_op jit(solution)/shard_map/all_to_all | solution.py:404
  279.5 2.1 copy.22
  (42 shorter events, 3.4 us)
Async XLA Ops:
  6.5 76.7 %all-gather.3.cloned.1.call-start = ((), (), s32[]{:S(2)}) async-start(), calls=%async_computation.3 | async-start | bytes 9732096 | tf_op jit(solution)/shard_map/all_gather | solution.py:50
  12.6 5.5 %collective-permute-start = (f32[144,128]{1,0:T(8,128)}, f32[144,128]{1,0:T(8,128)S(1)}, u32[]{:S(2)}, u32[]{:S(2)}) collective-permute-start(f32[144,128]{1,0:T(8,128)} %get-tuple-element.23), channel_id=1, source_target_pairs={{0,2},{2,4},{4,6},{6,0},{1,3},{3,5},{5,7},{7,1},{8,10},{10,12},{12... | collective-permute-start | bytes 221192 | tf_op jit(solution)/shard_map/ppermute | solution.py:48
  14.8 3.4 %collective-permute-start.1 = (f32[144,128]{1,0:T(8,128)}, f32[144,128]{1,0:T(8,128)S(1)}, u32[]{:S(2)}, u32[]{:S(2)}) collective-permute-start(f32[144,128]{1,0:T(8,128)} %get-tuple-element.23), channel_id=1, source_target_pairs={{0,6},{2,0},{4,2},{6,4},{1,7},{3,1},{5,3},{7,5},{8,14},{10,8},{12,... | collective-permute-start | bytes 221192 | tf_op jit(solution)/shard_map/ppermute | solution.py:48
  16.2 5.1 %collective-permute-start.2 = (f32[144,128]{1,0:T(8,128)}, f32[144,128]{1,0:T(8,128)S(1)}, u32[]{:S(2)}, u32[]{:S(2)}) collective-permute-start(f32[144,128]{1,0:T(8,128)} %get-tuple-element.23), channel_id=1, source_target_pairs={{0,4},{2,6},{4,0},{6,2},{1,5},{3,7},{5,1},{7,3},{8,12},{10,14},{12... | collective-permute-start | bytes 221192 | tf_op jit(solution)/shard_map/ppermute | solution.py:48
  22.9 6.1 %copy-start.3 = (s32[768]{0:T(1024)S(1)}, s32[768]{0:T(1024)}, u32[]{:S(2)}) copy-start(s32[768]{0:T(1024)} %ids.1) | copy-start | bytes 9220
  22.9 6.2 %copy-start.4 = (f32[2,128,4]{1,2,0:T(4,128)S(1)}, f32[2,128,4]{1,2,0:T(4,128)}, u32[]{:S(2)}) copy-start(f32[2,128,4]{1,2,0:T(4,128)} %param.13) | copy-start | bytes 12292
  23.0 36.0 %all-to-all-start = ((f32[8,584,128]{2,1,0:T(8,128)}), f32[8,584,128]{2,1,0:T(8,128)S(1)}, u32[]{:S(2)}, u32[]{:S(2)}) async-start(f32[8,584,128]{2,1,0:T(8,128)} %get-tuple-element.18), calls=%async_computation | async-start | bytes 4784128 | tf_op jit(solution)/shard_map/all_to_all | solution.py:330
  26.7 3.0 %copy-start.2 = (f32[2,128,128]{2,1,0:T(8,128)S(1)}, f32[2,128,128]{2,1,0:T(8,128)}, u32[]{:S(2)}) copy-start(f32[2,128,128]{2,1,0:T(8,128)} %param.14) | copy-start | bytes 393220
  26.8 5.7 %copy-start.5 = (f32[2,128]{1,0:T(2,128)S(1)}, f32[2,128]{1,0:T(2,128)}, u32[]{:S(2)}) copy-start(f32[2,128]{1,0:T(2,128)} %gain.1) | copy-start | bytes 3076
  26.8 184.6 %all-gather.5.cloned.1.call-start = ((), (), s32[]{:S(2)}) async-start(), calls=%async_computation.4 | async-start | bytes 9510912 | tf_op jit(solution)/shard_map/all_gather | solution.py:58
  59.0 1.9 copy-start
  124.5 43.6 %all-to-all-start.1 = ((f32[128,40,128]{2,1,0:T(8,128)}), f32[128,40,128]{2,1,0:T(8,128)S(1)}, u32[]{:S(2)}, u32[]{:S(2)}) async-start(f32[128,40,128]{2,1,0:T(8,128)} %bitcast.43), calls=%async_computation.1 | async-start | bytes 5242880 | tf_op jit(solution)/shard_map/all_to_all | solution.py:376
  168.1 1.5 copy-start.1
Sparse Core Ops, SparseCore 0:
  23.1 60.1 all-gather.2
  124.6 86.6 all-gather.4

commit v5 on v4

--- a/solution.py
+++ b/solution.py
@@ -245,13 +245,11 @@
     chain = sum(jnp.where(place == t, chain_gain[1, t], 0.0) for t in range(HEADS))
     for t in range(PAIR):
         first = x_ref[...].reshape(N, 128) + attend(t, query, key, value, gate, bias, w_out, mixed)
-        line[t] = first
         here = step * PAIR + t
         for row in range(16):
-            for k in range(LINES):
-                pair_ref[pl.ds(row * 8 * SLOT + here * LINES + k, 8, stride=SLOT), :] = line[
-                    t, pl.ds(row * LINES + k, 8, stride=96), :
-                ]
+            for col in range(8):
+                from_row = col * 96 + row * LINES
+                pair_ref[pl.ds((row * 8 + col) * SLOT + here * LINES, LINES), :] = first[from_row : from_row + LINES, :]
         normed = layer_norm(first, end_gain[...])
         plane = lax.dot_general(
             w_bias[...], normed, NT, precision=lax.Precision.HIGHEST, preferred_element_type=F32

time: 289 us -> 288 us (level)
  no operation moved by 1% of the time
where the time goes in v5:
time: 288 us; the launch traced here: 287 us
  waiting for transfers between devices  105 us (36%)
  Pallas kernels  99.1 us (34%)
  blocking collectives  35.7 us (12%)
  starting transfers between devices  16.6 us (6%)
  between operations  13.6 us (5%)
  local copies, waits for them, and re-layouts  9.53 us (3%)
  other arithmetic  7.84 us (3%)
    pallas_call x1, Pallas kernels, local(): pl.pallas_call(start_kernel, grid=(LINES // PAIR,), out_shape=(jax.ShapeD...  39.8 us
    all_to_all x1, blocking collectives, local(): lax.all_to_all(second, ROW, split_axis=0, concat_axis=0, tiled=True)  35.7 us
    all_to_all x1, waiting for transfers between devices, local(): lax.all_to_all(first_pair.reshape(128, SLOT, 128), EVERY, split_axis=0, c...  32.6 us
    pallas_call x1, Pallas kernels, local(): pl.pallas_call(end_kernel, grid=(LINES // PAIR,), out_shape=jax.ShapeDtyp...  32.5 us
    all_gather x1, waiting for transfers between devices, gather_end(): lax.all_gather(shard, ('z', 'x_hi', 'x_lo', 'y', 'core'), axis=0, tiled=T...  31.2 us
    all_to_all x1, waiting for transfers between devices, local(): rows = lax.all_to_all(parts, COL, split_axis=0, concat_axis=0, tiled=True)  25.3 us
    all_gather x1, waiting for transfers between devices, gather_start(): lax.all_gather(blocks, ('z', 'x_hi', 'x_lo', 'core'), axis=0, tiled=True)  12.1 us
    pallas_call x1, Pallas kernels, local(): pl.pallas_call(end_project_kernel, grid=(LINES,), out_shape=PROJECTED_SHA...  10.5 us
  transfers between devices with their start and end apart: 7, of which 6 were waited for; matrix products, arithmetic and copies ran while one was open for 4% of the time, Pallas kernels for 7%

profile of v5, /device:TPU:1, one launch (start us, length us, event | category | flops | bytes accessed | tf_op | source)
XLA Modules:
  0.0 287.0 jit_solution(712516832016337497)
XLA Ops:
  6.5 6.1 %tile_bias.1 = (f32[144,128]{1,0:T(8,128)}, f32[8,584,128]{2,1,0:T(8,128)}) custom-call(s32[768]{0:T(1024)} %ids.1, f32[2,4]{1,0:T(2,128)} %chain_gain.3, f32[48,96,128]{2,1,0:T(8,128)} %pair_ref.1, s32[48,96]{1,0:T(8,128)} %mask_ref.1, f32[2,128]{1,0:T(2,128)} %gain.1, f32[2,4,128]{2,1,0:T(4,128)} %bitcast.47), custom_call_target="tpu_custom_call" | custom-call | tf_op jit(solution)/shard_map/tile_bias/pallas_call | solution.py:311
  12.6 2.1 collective-permute-start
  14.8 1.4 collective-permute-start.1
  16.2 1.6 collective-permute-start.2
  18.2 3.1 %collective-permute-done.2 = f32[144,128]{1,0:T(8,128)S(1)} collective-permute-done((f32[144,128]{1,0:T(8,128)}, f32[144,128]{1,0:T(8,128)S(1)}, u32[]{:S(2)}, u32[]{:S(2)}) %collective-permute-start.2) | collective-permute-done | bytes 73760 | tf_op jit(solution)/shard_map/ppermute | solution.py:48
  21.3 1.6 pad_maximum_fusion
  23.0 3.8 %all-to-all-start = ((f32[8,584,128]{2,1,0:T(8,128)}), f32[8,584,128]{2,1,0:T(8,128)S(1)}, u32[]{:S(2)}, u32[]{:S(2)}) async-start(f32[8,584,128]{2,1,0:T(8,128)} %get-tuple-element.18), calls=%async_computation | async-start | bytes 4784128 | tf_op jit(solution)/shard_map/all_to_all | solution.py:328
  27.0 1.1 fusion.4
  28.3 0.8 copy.19.w_key
  29.8 0.7 maximum_bitcast_fusion.w_query
  30.5 0.7 maximum_bitcast_fusion.1.w_value
  31.1 0.7 maximum_bitcast_fusion.2.w_gate
  31.8 0.7 pad_maximum_fusion.2.w_out
  33.0 0.7 compare_convert_fusion.same
  33.7 25.3 %all-to-all-done.x_ref.mask_ref = f32[8,584,128]{2,1,0:T(8,128)S(1)} async-done(((f32[8,584,128]{2,1,0:T(8,128)}), f32[8,584,128]{2,1,0:T(8,128)S(1)}, u32[]{:S(2)}, u32[]{:S(2)}) %all-to-all-start) | async-done | bytes 2392096 | tf_op jit(solution)/shard_map/all_to_all | solution.py:328
  59.2 0.7 copy.16
  60.9 10.2 %start_projections.1 = (bf16[6,4,128,768]{3,2,1,0:T(8,128)(2,1)}, bf16[6,4,768,128]{3,2,1,0:T(8,128)(2,1)}, bf16[6,4,80,768]{3,2,1,0:T(8,128)(2,1)}, f32[6,128,768]{2,1,0:T(8,128)}) custom-call(f32[8,584,128]{2,1,0:T(8,128)} %copy-done, f32[8,584,128]{2,1,0:T(8,128)} %copy-done, bf16[256,256]{1,0:T(8,128)(2,1)} %maximum_bitcast_fusion.w_query, ...), custom_call_target="tpu_custom_call" | custom-call | tf_op jit(solution)/shard_map/start_projections/pallas_call | solution.py:336
  71.1 12.1 %all-gather.3.cloned.1.call-done.gathered = f32[18432,128]{1,0:T(8,128)} async-done(((f32[576,128]{1,0:T(8,128)}), f32[18432,128]{1,0:T(8,128)}) %all-gather.3.cloned.1.call-update) | async-done | bytes 9437200 | tf_op jit(solution)/shard_map/all_gather | solution.py:50
  83.2 39.8 %start_attention.1 = (f32[5120,128]{1,0:T(8,128)}, f32[24,768]{1,0:T(8,128)}) custom-call(f32[8,584,128]{2,1,0:T(8,128)} %copy-done, f32[128,128]{1,0:T(8,128)} %pad.5.mask_ref, bf16[6,4,128,768]{3,2,1,0:T(8,128)(2,1)} %get-tuple-element.19.query, bf16[6,4,768,128]{3,2,1,0:T(8,128)(2,1)} %get-tuple-element.20.key, ...), custom_call_target="tpu_custom_call" | custom-call | tf_op jit(solution)/shard_map/start_attention/pallas_call | solution.py:349
  123.1 7.4 %all-to-all-start.1 = ((f32[128,40,128]{2,1,0:T(8,128)}), f32[128,40,128]{2,1,0:T(8,128)S(1)}, u32[]{:S(2)}, u32[]{:S(2)}) async-start(f32[128,40,128]{2,1,0:T(8,128)} %bitcast.43), calls=%async_computation.1 | async-start | bytes 5242880 | tf_op jit(solution)/shard_map/all_to_all | solution.py:374
  130.7 0.8 copy.21.w_key
  131.4 0.7 maximum_bitcast_fusion.3.w_query
  132.1 0.7 maximum_bitcast_fusion.4.w_value
  132.8 0.7 maximum_bitcast_fusion.5.w_gate
  133.5 0.7 pad_maximum_fusion.4.w_out
  134.1 32.6 %all-to-all-done.1 = f32[128,40,128]{2,1,0:T(8,128)S(1)} async-done(((f32[128,40,128]{2,1,0:T(8,128)}), f32[128,40,128]{2,1,0:T(8,128)S(1)}, u32[]{:S(2)}, u32[]{:S(2)}) %all-to-all-start.1) | async-done | bytes 2621472 | tf_op jit(solution)/shard_map/all_to_all | solution.py:374
  166.7 1.5 copy-done.1
  168.2 10.5 %end_projections.1 = (bf16[6,4,128,768]{3,2,1,0:T(8,128)(2,1)}, bf16[6,4,768,128]{3,2,1,0:T(8,128)(2,1)}, bf16[6,4,80,768]{3,2,1,0:T(8,128)(2,1)}, f32[6,128,768]{2,1,0:T(8,128)}, f32[6,768,128]{2,1,0:T(8,128)}) custom-call(f32[5120,128]{1,0:T(8,128)} %bitcast.41, bf16[256,256]{1,0:T(8,128)(2,1)} %maximum_bitcast_fusion.3.w_query, ...), custom_call_target="tpu_custom_call" | custom-call | tf_op jit(solution)/shard_map/end_projections/pallas_call | solution.py:377
  178.7 31.2 %all-gather.5.cloned.1.call-done.gathered = f32[3072,768]{1,0:T(8,128)} async-done(((f32[24,768]{1,0:T(8,128)}), f32[3072,768]{1,0:T(8,128)}) %all-gather.5.cloned.1.call-update) | async-done | bytes 9437200 | tf_op jit(solution)/shard_map/all_gather | solution.py:58
  209.9 32.5 %end_attention.1 = f32[16,6,48,128]{3,2,1,0:T(8,128)} custom-call(f32[6,768,128]{2,1,0:T(8,128)} %get-tuple-element.25.x_ref, bf16[6,4,128,768]{3,2,1,0:T(8,128)(2,1)} %get-tuple-element.26.query, bf16[6,4,768,128]{3,2,1,0:T(8,128)(2,1)} %get-tuple-element.27.key, bf16[6,4,80,768]{3,2,1,0:T(8,128)(2,1)} %get-tuple-element.28.value, ...), custom_call_target="tpu_custom_call" | custom-call | tf_op jit(solution)/shard_map/end_attention/pallas_call | solution.py:387
  242.4 35.7 %all_to_all.15 = f32[16,6,48,128]{3,2,1,0:T(8,128)S(1)} all-to-all(f32[16,6,48,128]{3,2,1,0:T(8,128)} %end_attention.1), channel_id=1, replica_groups=mesh['z'=4,'x_hi'=2,'core'=2,'y'=4,'x_lo'=2] {'z','x_hi','core'}, dimensions={0} | all-to-all | bytes 4718592 | tf_op jit(solution)/shard_map/all_to_all | solution.py:402
  278.1 2.1 copy.22
  (42 shorter events, 3.4 us)
Async XLA Ops:
  6.5 76.7 %all-gather.3.cloned.1.call-start = ((), (), s32[]{:S(2)}) async-start(), calls=%async_computation.3 | async-start | bytes 9732096 | tf_op jit(solution)/shard_map/all_gather | solution.py:50
  12.6 5.5 %collective-permute-start = (f32[144,128]{1,0:T(8,128)}, f32[144,128]{1,0:T(8,128)S(1)}, u32[]{:S(2)}, u32[]{:S(2)}) collective-permute-start(f32[144,128]{1,0:T(8,128)} %get-tuple-element.23), channel_id=1, source_target_pairs={{0,2},{2,4},{4,6},{6,0},{1,3},{3,5},{5,7},{7,1},{8,10},{10,12},{12... | collective-permute-start | bytes 221192 | tf_op jit(solution)/shard_map/ppermute | solution.py:48
  14.8 3.4 %collective-permute-start.1 = (f32[144,128]{1,0:T(8,128)}, f32[144,128]{1,0:T(8,128)S(1)}, u32[]{:S(2)}, u32[]{:S(2)}) collective-permute-start(f32[144,128]{1,0:T(8,128)} %get-tuple-element.23), channel_id=1, source_target_pairs={{0,6},{2,0},{4,2},{6,4},{1,7},{3,1},{5,3},{7,5},{8,14},{10,8},{12,... | collective-permute-start | bytes 221192 | tf_op jit(solution)/shard_map/ppermute | solution.py:48
  16.2 5.1 %collective-permute-start.2 = (f32[144,128]{1,0:T(8,128)}, f32[144,128]{1,0:T(8,128)S(1)}, u32[]{:S(2)}, u32[]{:S(2)}) collective-permute-start(f32[144,128]{1,0:T(8,128)} %get-tuple-element.23), channel_id=1, source_target_pairs={{0,4},{2,6},{4,0},{6,2},{1,5},{3,7},{5,1},{7,3},{8,12},{10,14},{12... | collective-permute-start | bytes 221192 | tf_op jit(solution)/shard_map/ppermute | solution.py:48
  22.9 6.1 %copy-start.3 = (s32[768]{0:T(1024)S(1)}, s32[768]{0:T(1024)}, u32[]{:S(2)}) copy-start(s32[768]{0:T(1024)} %ids.1) | copy-start | bytes 9220
  22.9 6.2 %copy-start.4 = (f32[2,128,4]{1,2,0:T(4,128)S(1)}, f32[2,128,4]{1,2,0:T(4,128)}, u32[]{:S(2)}) copy-start(f32[2,128,4]{1,2,0:T(4,128)} %param.13) | copy-start | bytes 12292
  23.0 36.0 %all-to-all-start = ((f32[8,584,128]{2,1,0:T(8,128)}), f32[8,584,128]{2,1,0:T(8,128)S(1)}, u32[]{:S(2)}, u32[]{:S(2)}) async-start(f32[8,584,128]{2,1,0:T(8,128)} %get-tuple-element.18), calls=%async_computation | async-start | bytes 4784128 | tf_op jit(solution)/shard_map/all_to_all | solution.py:328
  26.7 3.0 %copy-start.2 = (f32[2,128,128]{2,1,0:T(8,128)S(1)}, f32[2,128,128]{2,1,0:T(8,128)}, u32[]{:S(2)}) copy-start(f32[2,128,128]{2,1,0:T(8,128)} %param.14) | copy-start | bytes 393220
  26.8 5.7 %copy-start.5 = (f32[2,128]{1,0:T(2,128)S(1)}, f32[2,128]{1,0:T(2,128)}, u32[]{:S(2)}) copy-start(f32[2,128]{1,0:T(2,128)} %gain.1) | copy-start | bytes 3076
  26.8 183.2 %all-gather.5.cloned.1.call-start = ((), (), s32[]{:S(2)}) async-start(), calls=%async_computation.4 | async-start | bytes 9510912 | tf_op jit(solution)/shard_map/all_gather | solution.py:58
  59.0 1.9 copy-start
  123.1 43.6 %all-to-all-start.1 = ((f32[128,40,128]{2,1,0:T(8,128)}), f32[128,40,128]{2,1,0:T(8,128)S(1)}, u32[]{:S(2)}, u32[]{:S(2)}) async-start(f32[128,40,128]{2,1,0:T(8,128)} %bitcast.43), calls=%async_computation.1 | async-start | bytes 5242880 | tf_op jit(solution)/shard_map/all_to_all | solution.py:374
  166.7 1.5 copy-start.1
Sparse Core Ops, SparseCore 0:
  23.1 60.1 all-gather.2
  123.2 86.6 all-gather.4

commit v6 on v5

--- a/solution.py
+++ b/solution.py
@@ -108,13 +108,20 @@
                 bias[head, start : start + 24, :] = jnp.concatenate(rows, axis=0)
 
 
-def tile_kernel(ids, chain_gain, pair_ref, mask_ref, gain, w_bias, out_ref, parts_ref, normed):
+def tile_kernel(ids, chain_gain, pair_ref, mask_ref, gain, w_bias, out_ref, parts, normed, masks, sems):
     mask = jnp.concatenate([mask_ref[...].astype(F32), jnp.zeros((48, 32), F32)], axis=1)
+    size = LINES * 96
     for part in range(8):
         inside = slice(part * LINES, (part + 1) * LINES)
-        parts_ref[part, : LINES * 96] = pair_ref[inside].reshape(LINES * 96, 128)
-        parts_ref[part, LINES * 96 :] = jnp.concatenate([mask[inside], jnp.zeros((2, 128), F32)], axis=0)
-    normed[...] = layer_norm(pair_ref[...].reshape(48 * 96, 128), gain[:1])
+        masks[part] = jnp.concatenate([mask[inside], jnp.zeros((2, 128), F32)], axis=0)
+    copies = []
+    for part in range(8):
+        pairs = pair_ref.at[pl.ds(part * size, size)]
+        copies.append(pltpu.make_async_copy(pairs, parts.at[part, pl.ds(0, size)], sems.at[part]))
+        copies.append(pltpu.make_async_copy(masks.at[part], parts.at[part, pl.ds(size, 8)], sems.at[8 + part]))
+    for copy in copies:
+        copy.start()
+    normed[...] = layer_norm(pair_ref[...], gain[:1])
     lane = lax.broadcasted_iota(jnp.int32, (128, 128), 1)
     head = (lane // 16) % 4
     columns = jnp.concatenate([w_bias[0], w_bias[0]], axis=0).T
@@ -147,6 +154,8 @@
     for part in range(3):
         before = lax.rem(lax.axis_index(ROW) * 3 + part, 8)
         out_ref[part * 48 : part * 48 + 48] = pltpu.roll(total[part * 48 : part * 48 + 48], before * 16, 1)
+    for copy in copies:
+        copy.wait()
 
 
 def project(x, mask, w_query, w_key, w_value, w_gate, gain, query, key, value, gate):
@@ -236,9 +245,10 @@
     @pl.when(step == 0)
     def _():
         copies = fetch(gathered, held, sems)
-        pair_ref[...] = jnp.zeros_like(pair_ref)
         for group in range(16):
             pair_ref[pl.ds(group * 8 * SLOT + LINES * LINES, 8, stride=SLOT), :] = mask_ref[group * 8 : group * 8 + 8]
+            for unused in range(LINES * LINES + 1, SLOT):
+                pair_ref[pl.ds(group * 8 * SLOT + unused, 8, stride=SLOT), :] = jnp.zeros((8, 128), F32)
         order_tiles(copies, held, bias)
 
     place = lax.broadcasted_iota(jnp.int32, (8, 1), 0)
@@ -319,10 +329,15 @@
             pl.BlockSpec(memory_space=pltpu.VMEM),
             pl.BlockSpec(memory_space=pltpu.VMEM),
         ],
-        scratch_shapes=[pltpu.VMEM((48 * 96, 128), F32)],
+        out_specs=(pl.BlockSpec(memory_space=pltpu.VMEM), pl.BlockSpec(memory_space=pl.ANY)),
+        scratch_shapes=[
+            pltpu.VMEM((48 * 96, 128), F32),
+            pltpu.VMEM((8, 8, 128), F32),
+            pltpu.SemaphoreType.DMA((16,)),
+        ],
         compiler_params=PARAMS,
         name="tile_bias",
-    )(chain_ids, chain_gain, pair_state, pair_mask, ln_gain, jnp.swapaxes(w_bias, 1, 2))
+    )(chain_ids, chain_gain, pair_state.reshape(48 * 96, 128), pair_mask, ln_gain, jnp.swapaxes(w_bias, 1, 2))
     start_bias = gather_start(tile_bias)
 
     rows = lax.all_to_all(parts, COL, split_axis=0, concat_axis=0, tiled=True)

time: 288 us -> 288 us (level)
  no operation moved by 1% of the time
where the time goes in v6:
time: 288 us
  waiting for transfers between devices  105 us (36%)
  Pallas kernels  99.7 us (35%)
  blocking collectives  35.7 us (12%)
  starting transfers between devices  16.5 us (6%)
  between operations  13.6 us (5%)
  local copies, waits for them, and re-layouts  9.54 us (3%)
  other arithmetic  7.84 us (3%)
    pallas_call x1, Pallas kernels, local(): pl.pallas_call(start_kernel, grid=(LINES // PAIR,), out_shape=(jax.ShapeD...  39.8 us
    all_to_all x1, blocking collectives, local(): lax.all_to_all(second, ROW, split_axis=0, concat_axis=0, tiled=True)  35.7 us
    all_to_all x1, waiting for transfers between devices, local(): lax.all_to_all(first_pair.reshape(128, SLOT, 128), EVERY, split_axis=0, c...  32.6 us
    pallas_call x1, Pallas kernels, local(): pl.pallas_call(end_kernel, grid=(LINES // PAIR,), out_shape=jax.ShapeDtyp...  32.5 us
    all_gather x1, waiting for transfers between devices, gather_end(): lax.all_gather(shard, ('z', 'x_hi', 'x_lo', 'y', 'core'), axis=0, tiled=T...  31.5 us
    all_to_all x1, waiting for transfers between devices, local(): rows = lax.all_to_all(parts, COL, split_axis=0, concat_axis=0, tiled=True)  25.5 us
    all_gather x1, waiting for transfers between devices, gather_start(): lax.all_gather(blocks, ('z', 'x_hi', 'x_lo', 'core'), axis=0, tiled=True)  12.1 us
    pallas_call x1, Pallas kernels, local(): pl.pallas_call(end_project_kernel, grid=(LINES,), out_shape=PROJECTED_SHA...  10.5 us
  transfers between devices with their start and end apart: 7, of which 6 were waited for; matrix products, arithmetic and copies ran while one was open for 4% of the time, Pallas kernels for 7%

profile of v6, /device:TPU:1, one launch (start us, length us, event | category | flops | bytes accessed | tf_op | source)
XLA Modules:
  0.0 287.9 jit_solution(9848765682109816975)
XLA Ops:
  6.5 6.6 %tile_bias.1 = (f32[144,128]{1,0:T(8,128)}, f32[8,584,128]{2,1,0:T(8,128)}) custom-call(s32[768]{0:T(1024)} %ids.1, f32[2,4]{1,0:T(2,128)} %chain_gain.3, f32[4608,128]{1,0:T(8,128)} %bitcast.45, s32[48,96]{1,0:T(8,128)} %mask_ref.1, f32[2,128]{1,0:T(2,128)} %gain.1, f32[2,4,128]{2,1,0:T(4,128)} %bitcast.49), custom_call_target="tpu_custom_call" | custom-call | tf_op jit(solution)/shard_map/tile_bias/pallas_call | solution.py:321
  13.2 2.2 collective-permute-start
  15.4 1.5 collective-permute-start.1
  16.9 1.6 collective-permute-start.2
  18.8 3.1 %collective-permute-done.2 = f32[144,128]{1,0:T(8,128)S(1)} collective-permute-done((f32[144,128]{1,0:T(8,128)}, f32[144,128]{1,0:T(8,128)S(1)}, u32[]{:S(2)}, u32[]{:S(2)}) %collective-permute-start.2) | collective-permute-done | bytes 73760 | tf_op jit(solution)/shard_map/ppermute | solution.py:48
  21.9 1.6 pad_maximum_fusion
  23.6 3.8 %all-to-all-start = ((f32[8,584,128]{2,1,0:T(8,128)}), f32[8,584,128]{2,1,0:T(8,128)S(1)}, u32[]{:S(2)}, u32[]{:S(2)}) async-start(f32[8,584,128]{2,1,0:T(8,128)} %get-tuple-element.18), calls=%async_computation | async-start | bytes 4784128 | tf_op jit(solution)/shard_map/all_to_all | solution.py:343
  27.4 1.1 fusion.4
  28.7 0.8 copy.19.w_key
  30.2 0.7 maximum_bitcast_fusion.w_query
  30.9 0.7 maximum_bitcast_fusion.1.w_value
  31.6 0.7 maximum_bitcast_fusion.2.w_gate
  32.2 0.7 pad_maximum_fusion.2.w_out
  33.4 0.7 compare_convert_fusion.same
  34.1 25.5 %all-to-all-done.x_ref.mask_ref = f32[8,584,128]{2,1,0:T(8,128)S(1)} async-done(((f32[8,584,128]{2,1,0:T(8,128)}), f32[8,584,128]{2,1,0:T(8,128)S(1)}, u32[]{:S(2)}, u32[]{:S(2)}) %all-to-all-start) | async-done | bytes 2392096 | tf_op jit(solution)/shard_map/all_to_all | solution.py:343
  59.9 0.7 copy.16
  61.5 10.2 %start_projections.1 = (bf16[6,4,128,768]{3,2,1,0:T(8,128)(2,1)}, bf16[6,4,768,128]{3,2,1,0:T(8,128)(2,1)}, bf16[6,4,80,768]{3,2,1,0:T(8,128)(2,1)}, f32[6,128,768]{2,1,0:T(8,128)}) custom-call(f32[8,584,128]{2,1,0:T(8,128)} %copy-done, f32[8,584,128]{2,1,0:T(8,128)} %copy-done, bf16[256,256]{1,0:T(8,128)(2,1)} %maximum_bitcast_fusion.w_query, ...), custom_call_target="tpu_custom_call" | custom-call | tf_op jit(solution)/shard_map/start_projections/pallas_call | solution.py:351
  71.7 12.1 %all-gather.3.cloned.1.call-done.gathered = f32[18432,128]{1,0:T(8,128)} async-done(((f32[576,128]{1,0:T(8,128)}), f32[18432,128]{1,0:T(8,128)}) %all-gather.3.cloned.1.call-update) | async-done | bytes 9437200 | tf_op jit(solution)/shard_map/all_gather | solution.py:50
  83.8 39.8 %start_attention.1 = (f32[5120,128]{1,0:T(8,128)}, f32[24,768]{1,0:T(8,128)}) custom-call(f32[8,584,128]{2,1,0:T(8,128)} %copy-done, f32[128,128]{1,0:T(8,128)} %pad.5.mask_ref, bf16[6,4,128,768]{3,2,1,0:T(8,128)(2,1)} %get-tuple-element.19.query, bf16[6,4,768,128]{3,2,1,0:T(8,128)(2,1)} %get-tuple-element.20.key, ...), custom_call_target="tpu_custom_call" | custom-call | tf_op jit(solution)/shard_map/start_attention/pallas_call | solution.py:364
  123.7 7.4 %all-to-all-start.1 = ((f32[128,40,128]{2,1,0:T(8,128)}), f32[128,40,128]{2,1,0:T(8,128)S(1)}, u32[]{:S(2)}, u32[]{:S(2)}) async-start(f32[128,40,128]{2,1,0:T(8,128)} %bitcast.44), calls=%async_computation.1 | async-start | bytes 5242880 | tf_op jit(solution)/shard_map/all_to_all | solution.py:389
  131.3 0.8 copy.21.w_key
  132.1 0.7 maximum_bitcast_fusion.3.w_query
  132.7 0.7 maximum_bitcast_fusion.4.w_value
  133.4 0.7 maximum_bitcast_fusion.5.w_gate
  134.1 0.7 pad_maximum_fusion.4.w_out
  134.7 32.6 %all-to-all-done.1 = f32[128,40,128]{2,1,0:T(8,128)S(1)} async-done(((f32[128,40,128]{2,1,0:T(8,128)}), f32[128,40,128]{2,1,0:T(8,128)S(1)}, u32[]{:S(2)}, u32[]{:S(2)}) %all-to-all-start.1) | async-done | bytes 2621472 | tf_op jit(solution)/shard_map/all_to_all | solution.py:389
  167.3 1.5 copy-done.1
  168.8 10.5 %end_projections.1 = (bf16[6,4,128,768]{3,2,1,0:T(8,128)(2,1)}, bf16[6,4,768,128]{3,2,1,0:T(8,128)(2,1)}, bf16[6,4,80,768]{3,2,1,0:T(8,128)(2,1)}, f32[6,128,768]{2,1,0:T(8,128)}, f32[6,768,128]{2,1,0:T(8,128)}) custom-call(f32[5120,128]{1,0:T(8,128)} %bitcast.42, bf16[256,256]{1,0:T(8,128)(2,1)} %maximum_bitcast_fusion.3.w_query, ...), custom_call_target="tpu_custom_call" | custom-call | tf_op jit(solution)/shard_map/end_projections/pallas_call | solution.py:392
  179.3 31.5 %all-gather.5.cloned.1.call-done.gathered = f32[3072,768]{1,0:T(8,128)} async-done(((f32[24,768]{1,0:T(8,128)}), f32[3072,768]{1,0:T(8,128)}) %all-gather.5.cloned.1.call-update) | async-done | bytes 9437200 | tf_op jit(solution)/shard_map/all_gather | solution.py:58
  210.8 32.5 %end_attention.1 = f32[16,6,48,128]{3,2,1,0:T(8,128)} custom-call(f32[6,768,128]{2,1,0:T(8,128)} %get-tuple-element.25.x_ref, bf16[6,4,128,768]{3,2,1,0:T(8,128)(2,1)} %get-tuple-element.26.query, bf16[6,4,768,128]{3,2,1,0:T(8,128)(2,1)} %get-tuple-element.27.key, bf16[6,4,80,768]{3,2,1,0:T(8,128)(2,1)} %get-tuple-element.28.value, ...), custom_call_target="tpu_custom_call" | custom-call | tf_op jit(solution)/shard_map/end_attention/pallas_call | solution.py:402
  243.3 35.7 %all_to_all.15 = f32[16,6,48,128]{3,2,1,0:T(8,128)S(1)} all-to-all(f32[16,6,48,128]{3,2,1,0:T(8,128)} %end_attention.1), channel_id=1, replica_groups=mesh['z'=4,'x_hi'=2,'core'=2,'y'=4,'x_lo'=2] {'z','x_hi','core'}, dimensions={0} | all-to-all | bytes 4718592 | tf_op jit(solution)/shard_map/all_to_all | solution.py:417
  278.9 2.1 copy.22
  (42 shorter events, 3.3 us)
Async XLA Ops:
  6.5 77.3 %all-gather.3.cloned.1.call-start = ((), (), s32[]{:S(2)}) async-start(), calls=%async_computation.3 | async-start | bytes 9732096 | tf_op jit(solution)/shard_map/all_gather | solution.py:50
  13.2 5.6 %collective-permute-start = (f32[144,128]{1,0:T(8,128)}, f32[144,128]{1,0:T(8,128)S(1)}, u32[]{:S(2)}, u32[]{:S(2)}) collective-permute-start(f32[144,128]{1,0:T(8,128)} %get-tuple-element.23), channel_id=1, source_target_pairs={{0,2},{2,4},{4,6},{6,0},{1,3},{3,5},{5,7},{7,1},{8,10},{10,12},{12... | collective-permute-start | bytes 221192 | tf_op jit(solution)/shard_map/ppermute | solution.py:48
  15.4 3.4 %collective-permute-start.1 = (f32[144,128]{1,0:T(8,128)}, f32[144,128]{1,0:T(8,128)S(1)}, u32[]{:S(2)}, u32[]{:S(2)}) collective-permute-start(f32[144,128]{1,0:T(8,128)} %get-tuple-element.23), channel_id=1, source_target_pairs={{0,6},{2,0},{4,2},{6,4},{1,7},{3,1},{5,3},{7,5},{8,14},{10,8},{12,... | collective-permute-start | bytes 221192 | tf_op jit(solution)/shard_map/ppermute | solution.py:48
  16.9 5.0 %collective-permute-start.2 = (f32[144,128]{1,0:T(8,128)}, f32[144,128]{1,0:T(8,128)S(1)}, u32[]{:S(2)}, u32[]{:S(2)}) collective-permute-start(f32[144,128]{1,0:T(8,128)} %get-tuple-element.23), channel_id=1, source_target_pairs={{0,4},{2,6},{4,0},{6,2},{1,5},{3,7},{5,1},{7,3},{8,12},{10,14},{12... | collective-permute-start | bytes 221192 | tf_op jit(solution)/shard_map/ppermute | solution.py:48
  23.5 5.9 %copy-start.3 = (s32[768]{0:T(1024)S(1)}, s32[768]{0:T(1024)}, u32[]{:S(2)}) copy-start(s32[768]{0:T(1024)} %ids.1) | copy-start | bytes 9220
  23.6 6.0 %copy-start.4 = (f32[2,128,4]{1,2,0:T(4,128)S(1)}, f32[2,128,4]{1,2,0:T(4,128)}, u32[]{:S(2)}) copy-start(f32[2,128,4]{1,2,0:T(4,128)} %param.13) | copy-start | bytes 12292
  23.6 36.0 %all-to-all-start = ((f32[8,584,128]{2,1,0:T(8,128)}), f32[8,584,128]{2,1,0:T(8,128)S(1)}, u32[]{:S(2)}, u32[]{:S(2)}) async-start(f32[8,584,128]{2,1,0:T(8,128)} %get-tuple-element.18), calls=%async_computation | async-start | bytes 4784128 | tf_op jit(solution)/shard_map/all_to_all | solution.py:343
  27.4 2.8 copy-start.2
  27.4 5.5 %copy-start.5 = (f32[2,128]{1,0:T(2,128)S(1)}, f32[2,128]{1,0:T(2,128)}, u32[]{:S(2)}) copy-start(f32[2,128]{1,0:T(2,128)} %gain.1) | copy-start | bytes 3076
  27.4 183.4 %all-gather.5.cloned.1.call-start = ((), (), s32[]{:S(2)}) async-start(), calls=%async_computation.4 | async-start | bytes 9510912 | tf_op jit(solution)/shard_map/all_gather | solution.py:58
  59.6 1.9 copy-start
  123.7 43.6 %all-to-all-start.1 = ((f32[128,40,128]{2,1,0:T(8,128)}), f32[128,40,128]{2,1,0:T(8,128)S(1)}, u32[]{:S(2)}, u32[]{:S(2)}) async-start(f32[128,40,128]{2,1,0:T(8,128)} %bitcast.44), calls=%async_computation.1 | async-start | bytes 5242880 | tf_op jit(solution)/shard_map/all_to_all | solution.py:389
  167.3 1.5 copy-start.1
Sparse Core Ops, SparseCore 0:
  23.7 60.1 all-gather.2
  123.8 86.9 all-gather.4
